TPU v7x, 32 devices: a whole 2x2x4 slice. The times are simulated.
32 devices in a mesh: section: 2 (over x), tm: 4 (over y, core), dp: 4 (over z).
Axes of the slice: x: 2, y: 2, z: 4, core: 2. Of those that a mesh axis runs over, the one named last changes fastest.
Arguments:
- frames: bfloat16 [8, 2048, 512], P(('section', 'dp'), 'tm'), may hold values from -6 to 6
- lengths: int32 [8], P(('section', 'dp')), may hold values from 10240 to 40960, as said below
- fourth_conv: bfloat16 [3, 512, 512], P(None, ('section', 'dp')), may hold values from -0.15625 to 0.15625
- fifth_conv: bfloat16 [3, 512, 512], P(None, ('section', 'dp')), may hold values from -0.15625 to 0.15625
- sixth_conv: bfloat16 [2, 512, 512], P(None, ('section', 'dp')), may hold values from -0.1875 to 0.1875
- seventh_conv: bfloat16 [2, 512, 512], P(None, ('section', 'dp')), may hold values from -0.1875 to 0.1875
- norm_gain: float32 [512], replicated, may hold values from 0.5 to 1.5
- norm_bias: float32 [512], replicated, may hold values from -1.8 to 1.8
- project_weight: bfloat16 [512, 480], P(None, 'tm'), may hold values from -0.25 to 0.25
- project_bias: bfloat16 [1, 480], P(None, 'tm'), may hold values from -1.796875 to 1.796875
- position_weight: bfloat16 [4, 128, 14400], P('tm', ('section', 'dp')), may hold values from -0.046875 to 0.046875
- position_bias: float32 [480], P('tm'), may hold values from -3 to 3
Outputs:
- encoded: bfloat16 [8, 480, 128], P(('section', 'dp'), 'tm')
Inputs may be any that keep to these rules, and one draw needn't show every extreme that they name: `lengths`: length of each utterance in samples; some utterance of every draw fills all 2048 input frames.
All inputs are finite; a program needn't handle non-finite values.
Results may differ from a plain program's by a relative error of at most 0.012.
Values may be sent and summed in bfloat16 or wider, within the bound.
No kernel may reach another device: no remote copies, remote signals or barrier semaphores. Data moves between devices by JAX's collectives and lax.ppermute only.
A program may use at most 64 MiB of HBM per device.

v0:
```python
import jax
import jax.numpy as jnp
from jax import lax
from jax.sharding import PartitionSpec as P

TAPS = 128


eps_norm = 1e-05


def passed_along(x, axis, by):
    length = lax.axis_size(axis)
    pairs = [(i, i + by) for i in range(length) if 0 <= i + by < length]
    return lax.ppermute(x, axis, pairs)


def layer_norm(values):
    average = jnp.mean(values, axis=-1, keepdims=True)
    centred = values - average
    spread = jnp.mean(centred * centred, axis=-1, keepdims=True)
    return centred * lax.rsqrt(spread + eps_norm)


def conv_layer(even_rows, odd_rows, weight, out_rows):
    tap_count = weight.shape[0]
    whole = lax.all_gather(weight, ("section", "dp"), axis=1, tiled=True)
    summed = jnp.dot(even_rows[:out_rows], whole[0], preferred_element_type=jnp.float32)
    summed = summed + jnp.dot(odd_rows[:out_rows], whole[1], preferred_element_type=jnp.float32)
    if tap_count == 3:
        summed = summed + jnp.dot(
            even_rows[1 : out_rows + 1], whole[2], preferred_element_type=jnp.float32
        )
    return jax.nn.gelu(layer_norm(summed), approximate=False).astype(jnp.bfloat16)


def paired_conv(current, weight, out_rows):
    paired = current.reshape(current.shape[0] // 2, 2, current.shape[1])
    return conv_layer(paired[:, 0], paired[:, 1], weight, out_rows)


def local(
    frames,
    lengths,
    fourth_conv,
    fifth_conv,
    sixth_conv,
    seventh_conv,
    norm_gain,
    norm_bias,
    project_weight,
    project_bias,
    position_weight,
    position_bias,
):
    inputs = frames[0]
    length = lengths[0]
    row_count = inputs.shape[0]
    channels = inputs.shape[1]
    sample_index = lax.axis_index("tm") * row_count + jnp.arange(row_count, dtype=jnp.int32)
    masked = jnp.where((sample_index * 20 < length)[:, None], inputs, jnp.zeros_like(inputs))
    zero_row = jnp.zeros((1, channels), jnp.bfloat16)
    current = masked
    for weight in (fourth_conv, fifth_conv, sixth_conv, seventh_conv):
        if weight.shape[0] == 3:
            next_rim = passed_along(current[:1], "tm", -1)
        else:
            next_rim = zero_row
        padded = jnp.concatenate([current, next_rim, zero_row], axis=0)
        current = paired_conv(padded, weight, current.shape[0] // 2)
    normed = (layer_norm(current.astype(jnp.float32)) * norm_gain + norm_bias).astype(jnp.bfloat16)
    grouped = (
        jnp.dot(
            lax.all_gather(normed, "tm", axis=0, tiled=True),
            project_weight,
            preferred_element_type=jnp.float32,
        )
        + project_bias.astype(jnp.float32)
    ).astype(jnp.bfloat16)
    frame_total = grouped.shape[0]
    group_width = grouped.shape[1]
    frame_index = jnp.arange(frame_total, dtype=jnp.int32)
    grouped = jnp.where((frame_index * 320 < length)[:, None], grouped, jnp.zeros_like(grouped))
    pad_rows = TAPS // 2
    padded_group = jnp.pad(grouped, ((pad_rows, pad_rows), (0, 0)))
    zeros_conv = jnp.zeros((group_width, frame_total), jnp.float32)
    shard_piece = lax.all_gather(position_weight, ("section", "dp"), axis=1, tiled=True)
    tap_total = shard_piece.shape[1]
    block_taps = min(tap_total, 16)
    kernel = shard_piece[0].reshape(tap_total, group_width, group_width)

    def one_block(counter, partial_value):
        base_tap = counter * block_taps
        window = jnp.concatenate(
            [
                lax.dynamic_slice_in_dim(padded_group, base_tap + offset, frame_total, 0)
                for offset in range(block_taps)
            ],
            axis=1,
        )
        window = window.reshape(frame_total, block_taps, group_width)
        tap_weights = lax.dynamic_slice_in_dim(kernel, counter * block_taps, block_taps, 0)
        return partial_value + lax.dot_general(
            tap_weights, window, (((0, 2), (1, 2)), ((), ())), preferred_element_type=jnp.float32
        )

    conv = lax.fori_loop(0, tap_total // block_taps, one_block, zeros_conv)
    position = jax.nn.gelu(conv + position_bias[:, None], approximate=False)
    encoded = (grouped.astype(jnp.float32).T + position).astype(jnp.bfloat16)
    return encoded[None]


def solution(mesh):
    in_specs = (
        P(("section", "dp"), "tm", None),
        P(("section", "dp")),
        P(None, ("section", "dp"), None),
        P(None, ("section", "dp"), None),
        P(None, ("section", "dp"), None),
        P(None, ("section", "dp"), None),
        P(),
        P(),
        P(None, "tm"),
        P(None, "tm"),
        P("tm", ("section", "dp"), None),
        P("tm"),
    )
    out_specs = P(("section", "dp"), "tm", None)
    return jax.shard_map(local, mesh=mesh, in_specs=in_specs, out_specs=out_specs, check_vma=False)
```

profile of v0, /device:TPU:0, one launch (start us, length us, event | category | flops | bytes accessed | tf_op | source)
XLA Modules:
  0.0 402.1 jit_solution(5335588336644720674)
XLA Ops:
  12.6 1.7 collective-permute-done
  15.6 40.8 %all-gather.6.cloned.1.call-done = bf16[3,512,512]{2,1,0:T(8,128)(2,1)} async-done(((bf16[3,64,512]{2,1,0:T(8,128)(2,1)}), bf16[3,512,512]{2,1,0:T(8,128)(2,1)}) %all-gather.6.cloned.1.call-update) | async-done | bytes 1572880 | tf_op jit(solution)/shard_map/all_gather | solution.py:27
  57.8 1.3 convolution_add_fusion.1
  59.1 1.4 fusion.78
  63.5 1.7 collective-permute-done.1
  65.8 35.4 %all-gather.8.cloned.1.call-done = bf16[3,512,512]{2,1,0:T(8,128)(2,1)} async-done(((bf16[3,64,512]{2,1,0:T(8,128)(2,1)}), bf16[3,512,512]{2,1,0:T(8,128)(2,1)}) %all-gather.8.cloned.1.call-update) | async-done | bytes 1572880 | tf_op jit(solution)/shard_map/all_gather | solution.py:27
  103.8 1.4 fusion.79
  106.4 36.1 %all-gather.10.cloned.1.call-done = bf16[2,512,512]{2,1,0:T(8,128)(2,1)} async-done(((bf16[2,64,512]{2,1,0:T(8,128)(2,1)}), bf16[2,512,512]{2,1,0:T(8,128)(2,1)}) %all-gather.10.cloned.1.call-update) | async-done | bytes 1048592 | tf_op jit(solution)/shard_map/all_gather | solution.py:27
  143.8 1.4 fusion.80
  145.9 37.6 %all-gather.12.cloned.1.call-done = bf16[2,512,512]{2,1,0:T(8,128)(2,1)} async-done(((bf16[2,64,512]{2,1,0:T(8,128)(2,1)}), bf16[2,512,512]{2,1,0:T(8,128)(2,1)}) %all-gather.12.cloned.1.call-update) | async-done | bytes 1048592 | tf_op jit(solution)/shard_map/all_gather | solution.py:27
  184.7 1.4 fusion.81
  186.9 5.4 %all_gather.22 = bf16[128,512]{1,0:T(8,128)(2,1)S(1)} all-gather(bf16[32,512]{1,0:T(8,128)(2,1)S(1)} %fusion.50), channel_id=1, replica_groups=mesh['section'=2,'tm'=4,'dp'=4] {'tm'}, dimensions={0}, use_global_device_ids=true | all-gather | bytes 163840 | tf_op jit(solution)/shard_map/all_gather | solution.py:74
  193.3 58.2 %all-gather.14.cloned.1.call-done = bf16[1,128,14400]{2,1,0:T(8,128)(2,1)} async-done(((bf16[1,16,14400]{2,1,0:T(8,128)(2,1)}), bf16[1,128,14400]{2,1,0:T(8,128)(2,1)}) %all-gather.14.cloned.1.call-update) | async-done | bytes 3686416 | tf_op jit(solution)/shard_map/all_gather | solution.py:87
  251.5 6.1 %copy.38 = bf16[1,128,14400]{1,2,0:T(8,128)(2,1)} copy(bf16[1,128,14400]{2,1,0:T(8,128)(2,1)} %all-gather.14.cloned.1.call-done) | data formatting | bytes 7372800 | tf_op jit(solution)/shard_map/all_gather | solution.py:87
  257.5 6.3 %copy.39 = bf16[128,120,120]{2,1,0:T(8,128)(2,1)} copy(bf16[128,120,120]{0,2,1:T(8,128)(2,1)} %bitcast.105) | data formatting | bytes 7372800
  263.8 131.0 %while.16 = (s32[]{:T(128)}, f32[120,128]{1,0:T(8,128)S(1)}, bf16[128,120,120]{2,1,0:T(8,128)(2,1)}, bf16[256,120]{0,1:T(8,128)(2,1)}, s32[]{:T(128)}, /*index=5...) while((s32[]{:T(128)}, f32[120,128]{1,0:T(8,128)S(1)}, ...), condition=%wide.region_11.12_spmd.clone, body=%wide.region_10.11_spmd.clone.sunk | while | flops 59013188 | bytes 2090124 | solution.py:107
  278.8 1.4 fusion.90
  295.1 1.4 fusion.90
  311.5 1.4 fusion.90
  327.9 1.4 fusion.90
  344.2 1.4 fusion.90
  360.6 1.4 fusion.90
  377.0 1.4 fusion.90
  393.4 1.4 fusion.90
  (198 shorter events, 139.1 us)
Async XLA Ops:
  6.5 185.8 %copy-start = (bf16[512,120]{0,1:T(8,128)(2,1)S(1)}, bf16[512,120]{0,1:T(8,128)(2,1)}, u32[]{:S(2)}) copy-start(bf16[512,120]{0,1:T(8,128)(2,1)} %param.22) | copy-start | bytes 368644
  6.5 6.0 %copy-start.4 = (bf16[1,120]{1,0:T(2,128)(2,1)S(1)}, bf16[1,120]{1,0:T(2,128)(2,1)}, u32[]{:S(2)}) copy-start(bf16[1,120]{1,0:T(2,128)(2,1)} %param.23) | copy-start | bytes 724
  6.5 49.9 %all-gather.6.cloned.1.call-start = ((), (), s32[]{:S(2)}) async-start(), calls=%async_computation | async-start | bytes 1769472 | tf_op jit(solution)/shard_map/all_gather | solution.py:27
  7.3 94.0 %all-gather.8.cloned.1.call-start = ((), (), s32[]{:S(2)}) async-start(), calls=%async_computation.1 | async-start | bytes 1769472 | tf_op jit(solution)/shard_map/all_gather | solution.py:27
  8.0 134.5 %all-gather.10.cloned.1.call-start = ((), (), s32[]{:S(2)}) async-start(), calls=%async_computation.2 | async-start | bytes 1179648 | tf_op jit(solution)/shard_map/all_gather | solution.py:27
  8.7 174.7 %all-gather.12.cloned.1.call-start = ((), (), s32[]{:S(2)}) async-start(), calls=%async_computation.3 | async-start | bytes 1179648 | tf_op jit(solution)/shard_map/all_gather | solution.py:27
  9.3 242.1 %all-gather.14.cloned.1.call-start = ((), (), s32[]{:S(2)}) async-start(), calls=%async_computation.4 | async-start | bytes 4165632 | tf_op jit(solution)/shard_map/all_gather | solution.py:87
  11.2 3.1 collective-permute-start
  62.1 3.1 collective-permute-start.1
  143.7 43.1 %copy-start.1 = (f32[512]{0:T(512)S(1)}, f32[512]{0:T(512)}, u32[]{:S(2)}) copy-start(f32[512]{0:T(512)} %param.21) | copy-start | bytes 6148
  143.7 43.1 %copy-start.2 = (f32[512]{0:T(512)S(1)}, f32[512]{0:T(512)}, u32[]{:S(2)}) copy-start(f32[512]{0:T(512)} %param.20) | copy-start | bytes 6148
  263.8 131.0 %copy-start.3 = (f32[120]{0:T(128)S(1)}, f32[120]{0:T(128)}, u32[]{:S(2)}) copy-start(f32[120]{0:T(128)} %param.25) | copy-start | bytes 1444
Sparse Core Ops, SparseCore 0:
  9.5 46.8 all-gather.5
  58.6 42.6 all-gather.7
  103.4 39.0 all-gather.9
  144.5 38.9 all-gather.11
  185.4 65.9 all-gather.13
where the time goes:
time: 410 us; the launch traced here: 402 us
  waiting for transfers between devices  214 us (52%)
  local copies, waits for them, and re-layouts  134 us (33%)
  matrix products  24.6 us (6%)
  between operations  14.1 us (3%)
  other arithmetic  5.92 us (1%)
  blocking collectives  5.43 us (1%)
    all_gather x4, waiting for transfers between devices, conv_layer(): whole = lax.all_gather(weight, ('section', 'dp'), axis=1, tiled=True)  150 us
    while x120, local copies, waits for them, and re-layouts  111 us
    all_gather x1, waiting for transfers between devices, local(): lax.all_gather(position_weight, ('section', 'dp'), axis=1, tiled=True)  58.2 us
    dot_general x8, matrix products, one_block(): lax.dot_general(tap_weights, window, (((0, 2), (1, 2)), ((), ())), prefer...  11.2 us
  transfers between devices with their start and end apart: 7, of which 7 were waited for; matrix products, arithmetic and copies ran while one was open for 5% of the time, Pallas kernels for 0%

commit v1 on v0

v1 whole, which is shorter than its diff:
```python
import functools

import jax
import jax.numpy as jnp
from jax import lax
from jax.experimental import pallas as pl
from jax.experimental.pallas import tpu as pltpu
from jax.sharding import PartitionSpec as P

TAPS = 128
ROW_TILE = 16
LANES = 128
PHASES = 16
SHARDED = ("section", "dp")
eps_norm = 1e-05
f32 = jnp.float32
bf16 = jnp.bfloat16


def bits_of(size):
    return [1 << b for b in range(size.bit_length() - 1)]


def swapped(x, axis, bit):
    return lax.ppermute(x, axis, [(i, i ^ bit) for i in range(lax.axis_size(axis))])


def swapped_by_parity(x, section_bit, tm_bit, section_first):
    sections, shares = lax.axis_size("section"), lax.axis_size("tm")
    pairs = []
    for s in range(sections):
        for t in range(shares):
            over_section = (t % 2 == 0) == section_first
            to = (s ^ section_bit, t) if over_section else (s, t ^ tm_bit)
            pairs.append((s * shares + t, to[0] * shares + to[1]))
    return lax.ppermute(x, ("section", "tm"), pairs)


def flipped(where, axis, bit):
    return tuple(w ^ (bit if name == axis else 0) for w, name in zip(where, ("section", "dp", "tm"), strict=True))


def gather_weights(own, parts):
    here = (0, 0, 0)
    distances = list(range(lax.axis_size("dp")))
    received = [own] + [swapped(own, "dp", k) for k in distances[1:]]
    pieces = []
    for k in range(0, len(received), 2):
        pair = received[k : k + 2]
        origins = [flipped(here, "dp", d) for d in distances[k : k + 2]]
        pieces.append((jnp.stack(pair), [(o, o) for o in origins]))
    section_bits = bits_of(lax.axis_size("section"))
    mixed = parts == 4 and section_bits
    for bit in section_bits[: -1 if mixed else None]:
        pieces += [
            (swapped(x, "section", bit), [(flipped(e, "section", bit), flipped(o, "section", bit)) for e, o in origins])
            for x, origins in pieces
        ]
    if mixed:
        bit = section_bits[-1]
        first = [
            (swapped_by_parity(x, bit, 2, True), [(flipped(e, "section", bit), flipped(o, "tm", 2)) for e, o in origins])
            for x, origins in pieces
        ]
        both = pieces + first
        second = [
            (swapped_by_parity(x, bit, 2, False), [(flipped(e, "tm", 2), flipped(o, "section", bit)) for e, o in origins])
            for x, origins in both
        ]
        pieces = both + second
    elif parts == 4:
        pieces += [
            (swapped(x, "tm", 2), [(flipped(e, "tm", 2), flipped(o, "tm", 2)) for e, o in origins]) for x, origins in pieces
        ]
    if parts >= 2:
        pieces += [
            (swapped(x, "tm", 1), [(flipped(o, "tm", 1), flipped(e, "tm", 1)) for e, o in origins]) for x, origins in pieces
        ]
    return [x for x, _ in pieces], [origin for _, origins in pieces for origin in origins]


def weight_rows(origins, parts, shard_rows):
    odd = lax.axis_index("tm") % 2
    picked = jnp.where(odd == 1, jnp.array([o for _, o in origins]), jnp.array([e for e, _ in origins]))
    section = lax.axis_index("section") ^ picked[:, 0]
    stage = lax.axis_index("dp") ^ picked[:, 1]
    part = (lax.axis_index("tm") % parts) ^ picked[:, 2]
    shard = section * lax.axis_size("dp") + stage
    return (shard * shard_rows + part * (shard_rows // parts)).astype(jnp.int32)


def layer_norm(values):
    average = jnp.mean(values, axis=-1, keepdims=True)
    centred = values - average
    spread = jnp.mean(centred * centred, axis=-1, keepdims=True)
    return centred * lax.rsqrt(spread + eps_norm)


def gelu(values):
    return 0.5 * values * (1.0 + lax.erf(values * (0.5**0.5)))


def dot(a, b):
    return jnp.dot(a, b, preferred_element_type=f32)


def dot_nt(a, b):
    return lax.dot_general(a, b, (((1,), (1,)), ((), ())), preferred_element_type=f32)


def put_rows(rows_ref, start, values):
    values = values.astype(f32)
    for block in range(rows_ref.shape[0]):
        rows_ref[block, pl.ds(start, values.shape[0]), :] = values[:, block * LANES : (block + 1) * LANES]


def strided_conv(rows_ref, weight_ref, out_rows):
    summed = None
    for tap in range(weight_ref.shape[0]):
        picked = jnp.concatenate(
            [rows_ref[block, pl.ds(tap, out_rows, stride=2), :].astype(bf16) for block in range(rows_ref.shape[0])],
            axis=1,
        )
        term = dot(picked, weight_ref[tap])
        summed = term if summed is None else summed + term
    return gelu(layer_norm(summed)).astype(bf16)


def start_assembly(piece_refs, first_rows, tap_slices, weight_refs, sems):
    for layer, (low, high) in enumerate(tap_slices):
        for index, piece in enumerate(piece_refs):
            slots, rows = piece.shape[0], piece.shape[2]
            for slot in range(slots):
                row = pl.multiple_of(first_rows[index * slots + slot], ROW_TILE)
                pltpu.make_async_copy(
                    piece.at[slot, low:high],
                    weight_refs[layer].at[:, pl.ds(row, rows), :],
                    sems.at[layer],
                ).start()


def wait_assembly(weight_ref, sem):
    pltpu.make_async_copy(weight_ref, weight_ref, sem).wait()


def front_kernel(n_pieces, tap_slices, first_rows, scalars, frames, halo, *rest):
    pieces, out = rest[:n_pieces], rest[n_pieces]
    w_a, w_b, x_in, x_mid, sems = rest[n_pieces + 1 :]
    start_assembly(pieces, first_rows, tap_slices, (w_a, w_b), sems)
    length, first = scalars[0], scalars[1]
    rows, halo_rows = frames.shape[0], halo.shape[0]
    channels = frames.shape[1]

    def masked(values, start):
        index = lax.broadcasted_iota(jnp.int32, (values.shape[0], 1), 0) + start
        return jnp.where(index * 20 < length, values.astype(f32), 0.0)

    put_rows(x_in, 0, masked(frames[...], first))
    put_rows(x_in, rows, masked(halo[...], first + rows))
    put_rows(x_in, rows + halo_rows, jnp.zeros((x_in.shape[1] - rows - halo_rows, channels), f32))
    wait_assembly(w_a, sems.at[0])
    put_rows(x_mid, 0, strided_conv(x_in, w_a, x_mid.shape[1]))
    wait_assembly(w_b, sems.at[1])
    out[...] = strided_conv(x_mid, w_b, out.shape[0])


def back_kernel(n_pieces, n_rows, tap_slices, first_rows, scalars, gain, bias, project, project_bias, *rest):
    pieces, row_pieces, out = rest[:n_pieces], rest[n_pieces : n_pieces + n_rows], rest[n_pieces + n_rows]
    w_a, w_b, x_in, x_mid, sems = rest[n_pieces + n_rows + 1 :]
    start_assembly(pieces, first_rows, tap_slices, (w_a, w_b), sems)
    length, tm = scalars[0], scalars[2]
    for index, piece in enumerate(row_pieces):
        rows = piece.shape[0]
        put_rows(x_in, pl.multiple_of((tm ^ index) * rows, ROW_TILE), piece[...])
    wait_assembly(w_a, sems.at[0])
    put_rows(x_mid, 0, strided_conv(x_in, w_a, x_mid.shape[1]))
    wait_assembly(w_b, sems.at[1])
    frames, group = out.shape[0], project.shape[0]
    extracted = strided_conv(x_mid, w_b, frames).astype(f32)
    normed = (layer_norm(extracted) * gain[...] + bias[...]).astype(bf16)
    hidden = (dot_nt(normed, project[...]) + project_bias[...].astype(f32)).astype(bf16)
    index = lax.broadcasted_iota(jnp.int32, (frames, 1), 0)
    hidden = jnp.where(index * 320 < length, hidden.astype(f32), 0.0)
    out[...] = jnp.zeros(out.shape, bf16)
    out[:, 0:group] = hidden.astype(bf16)


def position_kernel(n_pieces, offsets, hidden, *rest):
    pieces, out, padded, phases = rest[:n_pieces], rest[n_pieces], rest[n_pieces + 1], rest[n_pieces + 2]
    frames = hidden.shape[0]
    padded[...] = jnp.zeros(padded.shape, f32)
    padded[TAPS // 2 : TAPS // 2 + frames, :] = hidden[...].astype(f32)
    taps, width = pieces[0].shape[0], pieces[0].shape[1]
    span = phases.shape[0]
    for index, piece in enumerate(pieces):
        window = padded[pl.ds(offsets[index], span), :].astype(bf16)
        term = dot_nt(window, piece[...].reshape(taps * width, piece.shape[2]))
        if index == 0:
            phases[...] = term
        else:
            phases[...] += term
    total = phases[0:frames, 0:width]
    for tap in range(1, taps):
        total = total + phases[tap : tap + frames, tap * width : (tap + 1) * width]
    out[...] = total.astype(out.dtype)


def final_kernel(group, hidden, mine, theirs, bias, out):
    conv = mine[...] + theirs[...].astype(f32)
    encoded = hidden[...].astype(f32) + gelu(conv + bias[...])
    out[...] = jnp.transpose(encoded)[0:group, :].astype(bf16)


def vmem(count):
    return [pl.BlockSpec(memory_space=pltpu.VMEM)] * count


def smem(count):
    return [pl.BlockSpec(memory_space=pltpu.SMEM)] * count


def unplaced(count):
    return [pl.BlockSpec(memory_space=pl.ANY)] * count


LIMIT = pltpu.CompilerParams(vmem_limit_bytes=40 * 1024 * 1024)


def local(
    frames,
    lengths,
    fourth_conv,
    fifth_conv,
    sixth_conv,
    seventh_conv,
    norm_gain,
    norm_bias,
    project_weight,
    project_bias,
    position_weight,
    position_bias,
):
    sections, stages, shares = (lax.axis_size(a) for a in ("section", "dp", "tm"))
    section, stage, tm = (lax.axis_index(a) for a in ("section", "dp", "tm"))
    rows, channels = frames.shape[1:]
    shard_rows = fourth_conv.shape[1]
    parts = max(p for p in (1, 2, 4) if p <= shares and shard_rows % (p * ROW_TILE) == 0)
    part_rows = shard_rows // parts
    part = tm % parts

    def own_part(weights):
        return jnp.concatenate(
            [lax.dynamic_slice_in_dim(w, part * part_rows, part_rows, 1) for w in weights], axis=0
        )

    halo = lax.ppermute(frames[0, :ROW_TILE], "tm", [(i + 1, i) for i in range(shares - 1)])
    front_pieces, origins = gather_weights(own_part([fourth_conv, fifth_conv]), parts)
    back_pieces, _ = gather_weights(own_part([sixth_conv, seventh_conv]), parts)
    first_rows = weight_rows(origins, parts, shard_rows)
    scalars = jnp.stack([lengths[0], tm * rows, tm]).astype(jnp.int32)

    group = position_bias.shape[0]
    own_taps = position_weight.shape[1]
    taps = position_weight[0].reshape(own_taps, group, group)
    taps = jnp.pad(taps, ((0, 0), (0, LANES - group), (0, LANES - group)))
    tap_pieces, tap_places = [taps], [(0, 0, 0)]
    for axis, bits in (("section", bits_of(sections)), ("dp", bits_of(stages)[:-1])):
        for bit in bits:
            tap_pieces += [swapped(x, axis, bit) for x in tap_pieces]
            tap_places += [flipped(p, axis, bit) for p in tap_places]
    offsets = jnp.stack(
        [((section ^ p[0]) * stages + (stage ^ p[1])) * own_taps for p in tap_places]
    ).astype(jnp.int32)

    taps_of = [w.shape[0] for w in (fourth_conv, fifth_conv, sixth_conv, seventh_conv)]
    n_pieces = len(front_pieces)
    blocks = channels // LANES
    mid_rows = (rows // 2 + 8) // 8 * 8
    y_front = pl.pallas_call(
        functools.partial(front_kernel, n_pieces, [(0, taps_of[0]), (taps_of[0], taps_of[0] + taps_of[1])]),
        out_shape=jax.ShapeDtypeStruct((rows // 4, channels), bf16),
        in_specs=smem(2) + vmem(2) + unplaced(n_pieces),
        out_specs=pl.BlockSpec(memory_space=pltpu.VMEM),
        scratch_shapes=[
            pltpu.VMEM((taps_of[0], channels, channels), bf16),
            pltpu.VMEM((taps_of[1], channels, channels), bf16),
            pltpu.VMEM((blocks, rows + 2 * ROW_TILE, LANES), f32),
            pltpu.VMEM((blocks, mid_rows, LANES), f32),
            pltpu.SemaphoreType.DMA((2,)),
        ],
        compiler_params=LIMIT,
    )(first_rows, scalars, frames[0], halo, *front_pieces)

    row_pieces = [y_front]
    for bit in reversed(bits_of(shares)):
        row_pieces += [swapped(x, "tm", bit) for x in row_pieces]
    distance = [0]
    for bit in reversed(bits_of(shares)):
        distance += [d ^ bit for d in distance]
    row_pieces = [x for _, x in sorted(zip(distance, row_pieces), key=lambda pair: pair[0])]
    frame_total = rows * shares // 16

    hidden = pl.pallas_call(
        functools.partial(
            back_kernel, n_pieces, len(row_pieces), [(0, taps_of[2]), (taps_of[2], taps_of[2] + taps_of[3])]
        ),
        out_shape=jax.ShapeDtypeStruct((frame_total, LANES), bf16),
        in_specs=smem(2) + vmem(4) + unplaced(n_pieces) + vmem(len(row_pieces)),
        out_specs=pl.BlockSpec(memory_space=pltpu.VMEM),
        scratch_shapes=[
            pltpu.VMEM((taps_of[2], channels, channels), bf16),
            pltpu.VMEM((taps_of[3], channels, channels), bf16),
            pltpu.VMEM((blocks, rows * shares // 4, LANES), f32),
            pltpu.VMEM((blocks, rows * shares // 8, LANES), f32),
            pltpu.SemaphoreType.DMA((2,)),
        ],
        compiler_params=LIMIT,
    )(
        first_rows,
        scalars,
        norm_gain[None],
        norm_bias[None],
        project_weight.T,
        project_bias,
        *back_pieces,
        *row_pieces,
    )

    def partial_position(values, kind):
        return pl.pallas_call(
            functools.partial(position_kernel, len(tap_pieces)),
            out_shape=jax.ShapeDtypeStruct((frame_total, LANES), kind),
            in_specs=smem(1) + vmem(1 + len(tap_pieces)),
            out_specs=pl.BlockSpec(memory_space=pltpu.VMEM),
            scratch_shapes=[
                pltpu.VMEM((frame_total + TAPS, LANES), f32),
                pltpu.VMEM((frame_total + PHASES, own_taps * LANES), f32),
            ],
            compiler_params=LIMIT,
        )(offsets, values, *tap_pieces)

    far = stages // 2
    partner_hidden = swapped(hidden, "dp", far)
    mine = partial_position(hidden, f32)
    theirs = swapped(partial_position(partner_hidden, bf16), "dp", far)
    bias = jnp.pad(position_bias, (0, LANES - group))[None]
    encoded = pl.pallas_call(
        functools.partial(final_kernel, group),
        out_shape=jax.ShapeDtypeStruct((group, frame_total), bf16),
        in_specs=vmem(4),
        out_specs=pl.BlockSpec(memory_space=pltpu.VMEM),
    )(hidden, mine, theirs, bias)
    return encoded[None]


def solution(mesh):
    in_specs = (
        P(SHARDED, "tm", None),
        P(SHARDED),
        P(None, SHARDED, None),
        P(None, SHARDED, None),
        P(None, SHARDED, None),
        P(None, SHARDED, None),
        P(),
        P(),
        P(None, "tm"),
        P(None, "tm"),
        P("tm", SHARDED, None),
        P("tm"),
    )
    out_specs = P(SHARDED, "tm", None)
    return jax.shard_map(local, mesh=mesh, in_specs=in_specs, out_specs=out_specs, check_vma=False)
```

time: 410 us -> 113 us (0.28); the launches traced: 402 us -> 113 us
  waiting for transfers between devices: 214 us -> 33.2 us
  local copies, waits for them, and re-layouts: 134 us -> 22.9 us
  starting transfers between devices: 2.74 us -> 43.9 us
  matrix products: 24.6 us -> 0 us
  between operations: 14.1 us -> 0.97 us
  Pallas kernels: 0 us -> 10.9 us
  blocking collectives: 5.43 us -> 0 us
  other arithmetic: 5.92 us -> 0.79 us
    all_gather x5 -> x0, waiting for transfers between devices: 208 us -> none  [the longest x4 150 us: conv_layer(): whole = lax.all_gather(weight, ('section', 'dp'), axis=1, tiled=True)]
    while x120 -> x0, local copies, waits for them, and re-layouts: 111 us -> none
    ppermute x2 -> x43, starting transfers between devices: 2.58 us -> 43.9 us  [the longest x30 30.5 us: swapped(): lax.ppermute(x, axis, [(i, i ^ bit) for i in range(lax.axis_size(axis))])]
    ppermute x2 -> x43, waiting for transfers between devices: 3.43 us -> 33.2 us  [the longest x30 22.3 us: swapped(): lax.ppermute(x, axis, [(i, i ^ bit) for i in range(lax.axis_size(axis))])]
    dot_general x19 -> x0, matrix products: 24.6 us -> none  [the longest x8 11.2 us: one_block(): lax.dot_general(tap_weights, window, (((0, 2), (1, 2)), ((), ())), prefer...]
    unnamed x11 -> x80, local copies, waits for them, and re-layouts: 6.29 us -> 20 us
    pallas_call x0 -> x5, Pallas kernels: none -> 10.9 us  [the longest x1 3.41 us: local(): pl.pallas_call(functools.partial(front_kernel, n_pieces, [(0, taps_of[0])...]
    concatenate x10 -> x0, local copies, waits for them, and re-layouts: 7.42 us -> none  [the longest x8 7.4 us: one_block(): jnp.concatenate([lax.dynamic_slice_in_dim(padded_group, base_tap + offset...]
  transfers between devices with their start and end apart: 7 -> 43, of which waited for: 7 -> 11; matrix products, arithmetic and copies ran while one was open for 5% -> 3% of each run, Pallas kernels for 0% -> 7%
where the time goes in v1:
time: 113 us
  starting transfers between devices  43.9 us (39%)
  waiting for transfers between devices  33.2 us (29%)
  local copies, waits for them, and re-layouts  22.9 us (20%)
  Pallas kernels  10.9 us (10%)
    ppermute x30, starting transfers between devices, swapped(): lax.ppermute(x, axis, [(i, i ^ bit) for i in range(lax.axis_size(axis))])  30.5 us
    ppermute x30, waiting for transfers between devices, swapped(): lax.ppermute(x, axis, [(i, i ^ bit) for i in range(lax.axis_size(axis))])  22.3 us
    unnamed x80, local copies, waits for them, and re-layouts  20 us
    ppermute x12, starting transfers between devices, swapped_by_parity(): return lax.ppermute(x, ('section', 'tm'), pairs)  12.2 us
    ppermute x12, waiting for transfers between devices, swapped_by_parity(): return lax.ppermute(x, ('section', 'tm'), pairs)  10.8 us
    pallas_call x1, Pallas kernels, local(): pl.pallas_call(functools.partial(front_kernel, n_pieces, [(0, taps_of[0])...  3.41 us
    pallas_call x1, Pallas kernels, local(): pl.pallas_call(functools.partial(back_kernel, n_pieces, len(row_pieces),...  3.32 us
    pallas_call x2, Pallas kernels, partial_position(): pl.pallas_call(functools.partial(position_kernel, len(tap_pieces)), out_s...  2.65 us
  transfers between devices with their start and end apart: 43, of which 11 were waited for; matrix products, arithmetic and copies ran while one was open for 3% of the time, Pallas kernels for 7%

profile of v1, /device:TPU:0, one launch (start us, length us, event | category | flops | bytes accessed | tf_op | source)
XLA Modules:
  0.0 112.7 jit_solution(7332149323256988501)
XLA Ops:
  0.9 4.1 %collective-permute-start.19 = (bf16[6,16,512]{2,1,0:T(8,128)(2,1)S(1)}, bf16[6,16,512]{2,1,0:T(8,128)(2,1)S(1)}, u32[]{:S(2)}, u32[]{:S(2)}) collective-permute-start(bf16[6,16,512]{2,1,0:T(8,128)(2,1)S(1)} %get-tuple-element.6), channel_id=1, source_target_pairs={{0,2},{1,3},{2,0},{3,1},{4,6},{5,7},{6,4},{7,5},{8,10},{9,11},{10,... | collective-permute-start | bytes 294920 | tf_op jit(solution)/shard_map/ppermute | solution.py:25
  5.0 1.3 %collective-permute-start.20 = (bf16[6,16,512]{2,1,0:T(8,128)(2,1)S(1)}, bf16[6,16,512]{2,1,0:T(8,128)(2,1)S(1)}, u32[]{:S(2)}, u32[]{:S(2)}) collective-permute-start(bf16[6,16,512]{2,1,0:T(8,128)(2,1)S(1)} %get-tuple-element.6), channel_id=1, source_target_pairs={{0,3},{1,2},{2,1},{3,0},{4,7},{5,6},{6,5},{7,4},{8,11},{9,10},{10,... | collective-permute-start | bytes 294920 | tf_op jit(solution)/shard_map/ppermute | solution.py:25
  7.2 1.8 %collective-permute-start.1 = (bf16[4,16,512]{2,1,0:T(8,128)(2,1)S(1)}, bf16[4,16,512]{2,1,0:T(8,128)(2,1)S(1)}, u32[]{:S(2)}, u32[]{:S(2)}) collective-permute-start(bf16[4,16,512]{2,1,0:T(8,128)(2,1)S(1)} %get-tuple-element.8), channel_id=1, source_target_pairs={{0,2},{1,3},{2,0},{3,1},{4,6},{5,7},{6,4},{7,5},{8,10},{9,11},{10,... | collective-permute-start | bytes 196616 | tf_op jit(solution)/shard_map/ppermute | solution.py:25
  10.7 8.3 %collective-permute-done.1 = bf16[4,16,512]{2,1,0:T(8,128)(2,1)S(1)} collective-permute-done((bf16[4,16,512]{2,1,0:T(8,128)(2,1)S(1)}, bf16[4,16,512]{2,1,0:T(8,128)(2,1)S(1)}, u32[]{:S(2)}, u32[]{:S(2)}) %collective-permute-start.1) | collective-permute-done | bytes 65568 | tf_op jit(solution)/shard_map/ppermute | solution.py:25
  20.4 1.6 %collective-permute-start.4 = (bf16[2,4,16,512]{3,2,1,0:T(8,128)(2,1)S(1)}, bf16[2,4,16,512]{3,2,1,0:T(8,128)(2,1)S(1)}, u32[]{:S(2)}, u32[]{:S(2)}) collective-permute-start(bf16[2,4,16,512]{3,2,1,0:T(8,128)(2,1)S(1)} %pad_maximum_fusion.3.rest_1_), channel_id=1, source_target_pairs={{0,16},{4,12},{8,24},{12,4},{16,0},{20,28},{24,8},{28,20},{1,17},{... | collective-permute-start | bytes 393224 | tf_op jit(solution)/shard_map/ppermute | solution.py:36
  22.0 2.1 %collective-permute-start.6 = (bf16[2,4,16,512]{3,2,1,0:T(8,128)(2,1)S(1)}, bf16[2,4,16,512]{3,2,1,0:T(8,128)(2,1)}, u32[]{:S(2)}, u32[]{:S(2)}) collective-permute-start(bf16[2,4,16,512]{3,2,1,0:T(8,128)(2,1)S(1)} %pad_maximum_fusion.3.rest_1_), channel_id=1, source_target_pairs={{0,8},{4,20},{8,0},{12,28},{16,24},{20,4},{24,16},{28,12},{1,9},{5... | collective-permute-start | bytes 393224 | tf_op jit(solution)/shard_map/ppermute | solution.py:36
  24.4 1.4 %collective-permute-start.3 = (bf16[2,4,16,512]{3,2,1,0:T(8,128)(2,1)S(1)}, bf16[2,4,16,512]{3,2,1,0:T(8,128)(2,1)}, u32[]{:S(2)}, u32[]{:S(2)}) collective-permute-start(bf16[2,4,16,512]{3,2,1,0:T(8,128)(2,1)S(1)} %pad_maximum_fusion.2.rest_0_), channel_id=1, source_target_pairs={{0,16},{4,12},{8,24},{12,4},{16,0},{20,28},{24,8},{28,20},{1,17},{... | collective-permute-start | bytes 393224 | tf_op jit(solution)/shard_map/ppermute | solution.py:36
  25.9 3.2 %collective-permute-done.18 = bf16[6,16,512]{2,1,0:T(8,128)(2,1)S(1)} collective-permute-done((bf16[6,16,512]{2,1,0:T(8,128)(2,1)S(1)}, bf16[6,16,512]{2,1,0:T(8,128)(2,1)S(1)}, u32[]{:S(2)}, u32[]{:S(2)}) %collective-permute-start.18) | collective-permute-done | bytes 98336 | tf_op jit(solution)/shard_map/ppermute | solution.py:25
  30.7 1.8 %collective-permute-start.21 = (bf16[2,6,16,512]{3,2,1,0:T(8,128)(2,1)S(1)}, bf16[2,6,16,512]{3,2,1,0:T(8,128)(2,1)S(1)}, u32[]{:S(2)}, u32[]{:S(2)}) collective-permute-start(bf16[2,6,16,512]{3,2,1,0:T(8,128)(2,1)S(1)} %pad_maximum_fusion.rest_0_), channel_id=1, source_target_pairs={{0,16},{4,12},{8,24},{12,4},{16,0},{20,28},{24,8},{28,20},{1,17},{... | collective-permute-start | bytes 589832 | tf_op jit(solution)/shard_map/ppermute | solution.py:36
  33.3 1.9 %collective-permute-done.5.rest_4_ = bf16[2,4,16,512]{3,2,1,0:T(8,128)(2,1)} collective-permute-done((bf16[2,4,16,512]{3,2,1,0:T(8,128)(2,1)S(1)}, bf16[2,4,16,512]{3,2,1,0:T(8,128)(2,1)}, u32[]{:S(2)}, u32[]{:S(2)}) %collective-permute-start.5) | collective-permute-done | bytes 131104 | tf_op jit(solution)/shard_map/ppermute | solution.py:36
  36.0 1.6 %collective-permute-done.22.rest_3_ = bf16[2,6,16,512]{3,2,1,0:T(8,128)(2,1)S(1)} collective-permute-done((bf16[2,6,16,512]{3,2,1,0:T(8,128)(2,1)S(1)}, bf16[2,6,16,512]{3,2,1,0:T(8,128)(2,1)S(1)}, u32[]{:S(2)}, u32[]{:S(2)}) %collective-permute-start.22) | collective-permute-done | bytes 196640 | tf_op jit(solution)/shard_map/ppermute | solution.py:36
  37.5 4.2 %collective-permute-done.21.rest_2_ = bf16[2,6,16,512]{3,2,1,0:T(8,128)(2,1)S(1)} collective-permute-done((bf16[2,6,16,512]{3,2,1,0:T(8,128)(2,1)S(1)}, bf16[2,6,16,512]{3,2,1,0:T(8,128)(2,1)S(1)}, u32[]{:S(2)}, u32[]{:S(2)}) %collective-permute-start.21) | collective-permute-done | bytes 196640 | tf_op jit(solution)/shard_map/ppermute | solution.py:36
  47.5 3.1 %collective-permute-done.26.rest_7_ = bf16[2,6,16,512]{3,2,1,0:T(8,128)(2,1)S(1)} collective-permute-done((bf16[2,6,16,512]{3,2,1,0:T(8,128)(2,1)S(1)}, bf16[2,6,16,512]{3,2,1,0:T(8,128)(2,1)S(1)}, u32[]{:S(2)}, u32[]{:S(2)}) %collective-permute-start.26) | collective-permute-done | bytes 196640 | tf_op jit(solution)/shard_map/ppermute | solution.py:36
  50.6 8.7 %collective-permute-start.29 = (bf16[2,6,16,512]{3,2,1,0:T(8,128)(2,1)S(1)}, bf16[2,6,16,512]{3,2,1,0:T(8,128)(2,1)S(1)}, u32[]{:S(2)}, u32[]{:S(2)}) collective-permute-start(bf16[2,6,16,512]{3,2,1,0:T(8,128)(2,1)S(1)} %collective-permute-done.21.rest_2_), channel_id=1, source_target_pairs={{0,4},{4,0},{8,12},{12,8},{1,5},{5,1},{9,13},{13,9},{2,6},{6,2},{1... | collective-permute-start | bytes 589832 | tf_op jit(solution)/shard_map/ppermute | solution.py:25
  59.3 2.2 %collective-permute-start.31 = (bf16[2,6,16,512]{3,2,1,0:T(8,128)(2,1)S(1)}, bf16[2,6,16,512]{3,2,1,0:T(8,128)(2,1)S(1)}, u32[]{:S(2)}, u32[]{:S(2)}) collective-permute-start(bf16[2,6,16,512]{3,2,1,0:T(8,128)(2,1)S(1)} %collective-permute-done.23.rest_4_), channel_id=1, source_target_pairs={{0,4},{4,0},{8,12},{12,8},{1,5},{5,1},{9,13},{13,9},{2,6},{6,2},{1... | collective-permute-start | bytes 589832 | tf_op jit(solution)/shard_map/ppermute | solution.py:25
  65.0 1.3 %collective-permute-start.7 = (bf16[2,4,16,512]{3,2,1,0:T(8,128)(2,1)}, bf16[2,4,16,512]{3,2,1,0:T(8,128)(2,1)}, u32[]{:S(2)}, u32[]{:S(2)}) collective-permute-start(bf16[2,4,16,512]{3,2,1,0:T(8,128)(2,1)} %collective-permute-done.3.rest_2_), channel_id=1, source_target_pairs={{0,8},{4,20},{8,0},{12,28},{16,24},{20,4},{24,16},{28,12},{1,9},{5... | collective-permute-start | bytes 393224 | tf_op jit(solution)/shard_map/ppermute | solution.py:36
  68.3 2.0 %collective-permute-start.40 = (bf16[16,128,128]{2,1,0:T(8,128)(2,1)S(1)}, bf16[16,128,128]{2,1,0:T(8,128)(2,1)S(1)}, u32[]{:S(2)}, u32[]{:S(2)}) collective-permute-start(bf16[16,128,128]{2,1,0:T(8,128)(2,1)S(1)} %collective-permute-done.38.rest_1_), channel_id=1, source_target_pairs={{0,1},{1,0},{2,3},{3,2},{4,5},{5,4},{6,7},{7,6},{8,9},{9,8},{10,11... | collective-permute-start | bytes 1572872 | tf_op jit(solution)/shard_map/ppermute | solution.py:25
  81.5 3.4 %shard_map.136.rest_16_ = bf16[128,512]{1,0:T(8,128)(2,1)S(1)} custom-call(s32[32]{0:T(128)S(1)} %copy-done.28, s32[3]{0:T(128)S(1)} %pad_add_fusion.scalars, bf16[512,512]{1,0:T(8,128)(2,1)S(1)} %bitcast.27, bf16[16,512]{1,0:T(8,128)(2,1)S(1)} %collective-permute-done.17.halo, bf16[2,6,16,512]{3,2,1,0:T(8,128)(2,1)S(1)} %pad_maximum_fusion.rest_0_, ...), custom_call_target="tpu_custom_call" | custom-call | tf_op jit(solution)/shard_map/pallas_call | solution.py:279
  87.0 3.9 %collective-permute-done.36.rest_18_ = bf16[128,512]{1,0:T(8,128)(2,1)S(1)} collective-permute-done((bf16[128,512]{1,0:T(8,128)(2,1)S(1)}, bf16[128,512]{1,0:T(8,128)(2,1)S(1)}, u32[]{:S(2)}, u32[]{:S(2)}) %collective-permute-start.36) | collective-permute-done | bytes 131104 | tf_op jit(solution)/shard_map/ppermute | solution.py:25
  91.0 1.3 %collective-permute-done.37.rest_19_ = bf16[128,512]{1,0:T(8,128)(2,1)S(1)} collective-permute-done((bf16[128,512]{1,0:T(8,128)(2,1)S(1)}, bf16[128,512]{1,0:T(8,128)(2,1)S(1)}, u32[]{:S(2)}, u32[]{:S(2)}) %collective-permute-start.37) | collective-permute-done | bytes 131104 | tf_op jit(solution)/shard_map/ppermute | solution.py:25
  95.8 3.3 %shard_map.137.hidden = bf16[128,128]{1,0:T(8,128)(2,1)S(1)} custom-call(s32[32]{0:T(128)S(1)} %copy-done.29, s32[3]{0:T(128)S(1)} %copy-done.31, f32[1,512]{1,0:T(1,128)S(1)} %bitcast.29, f32[1,512]{1,0:T(1,128)S(1)} %bitcast.30, bf16[120,512]{1,0:T(8,128)(2,1)S(1)} %bitcast.28, bf16[1,120]{1,0:T(2,128)(2,1)S(1)} %copy-done.34, ...), custom_call_target="tpu_custom_call" | custom-call | tf_op jit(solution)/shard_map/pallas_call | solution.py:303
  99.1 1.5 %collective-permute-start.41 = (bf16[128,128]{1,0:T(8,128)(2,1)S(1)}, bf16[128,128]{1,0:T(8,128)(2,1)S(1)}, u32[]{:S(2)}, u32[]{:S(2)}) collective-permute-start(bf16[128,128]{1,0:T(8,128)(2,1)S(1)} %shard_map.137.hidden), channel_id=1, source_target_pairs={{0,2},{1,3},{2,0},{3,1},{4,6},{5,7},{6,4},{7,5},{8,10},{9,11},{10,... | collective-permute-start | bytes 98312 | tf_op jit(solution)/shard_map/ppermute | solution.py:25
  100.7 3.6 %collective-permute-done.41.hidden = bf16[128,128]{1,0:T(8,128)(2,1)S(1)} collective-permute-done((bf16[128,128]{1,0:T(8,128)(2,1)S(1)}, bf16[128,128]{1,0:T(8,128)(2,1)S(1)}, u32[]{:S(2)}, u32[]{:S(2)}) %collective-permute-start.41) | collective-permute-done | bytes 32800 | tf_op jit(solution)/shard_map/ppermute | solution.py:25
  111.1 1.6 %shard_map.140 = bf16[120,128]{1,0:T(8,128)(2,1)} custom-call(bf16[128,128]{1,0:T(8,128)(2,1)} %copy-done.1, f32[128,128]{1,0:T(8,128)} %copy-done.2, bf16[128,128]{1,0:T(8,128)(2,1)} %copy-done.36, f32[1,128]{1,0:T(1,128)} %pad_bitcast_fusion.bias), custom_call_target="tpu_custom_call" | custom-call | tf_op jit(solution)/shard_map/pallas_call | solution.py:347
  (163 shorter events, 42.2 us)
Async XLA Ops:
  0.9 23.4 %collective-permute-start.19 = (bf16[6,16,512]{2,1,0:T(8,128)(2,1)S(1)}, bf16[6,16,512]{2,1,0:T(8,128)(2,1)S(1)}, u32[]{:S(2)}, u32[]{:S(2)}) collective-permute-start(bf16[6,16,512]{2,1,0:T(8,128)(2,1)S(1)} %get-tuple-element.6), channel_id=1, source_target_pairs={{0,2},{1,3},{2,0},{3,1},{4,6},{5,7},{6,4},{7,5},{8,10},{9,11},{10,... | collective-permute-start | bytes 294920 | tf_op jit(solution)/shard_map/ppermute | solution.py:25
  5.0 19.4 %collective-permute-start.20 = (bf16[6,16,512]{2,1,0:T(8,128)(2,1)S(1)}, bf16[6,16,512]{2,1,0:T(8,128)(2,1)S(1)}, u32[]{:S(2)}, u32[]{:S(2)}) collective-permute-start(bf16[6,16,512]{2,1,0:T(8,128)(2,1)S(1)} %get-tuple-element.6), channel_id=1, source_target_pairs={{0,3},{1,2},{2,1},{3,0},{4,7},{5,6},{6,5},{7,4},{8,11},{9,10},{10,... | collective-permute-start | bytes 294920 | tf_op jit(solution)/shard_map/ppermute | solution.py:25
  7.2 11.9 %collective-permute-start.1 = (bf16[4,16,512]{2,1,0:T(8,128)(2,1)S(1)}, bf16[4,16,512]{2,1,0:T(8,128)(2,1)S(1)}, u32[]{:S(2)}, u32[]{:S(2)}) collective-permute-start(bf16[4,16,512]{2,1,0:T(8,128)(2,1)S(1)} %get-tuple-element.8), channel_id=1, source_target_pairs={{0,2},{1,3},{2,0},{3,1},{4,6},{5,7},{6,4},{7,5},{8,10},{9,11},{10,... | collective-permute-start | bytes 196616 | tf_op jit(solution)/shard_map/ppermute | solution.py:25
  8.9 11.4 %collective-permute-start.2 = (bf16[4,16,512]{2,1,0:T(8,128)(2,1)S(1)}, bf16[4,16,512]{2,1,0:T(8,128)(2,1)S(1)}, u32[]{:S(2)}, u32[]{:S(2)}) collective-permute-start(bf16[4,16,512]{2,1,0:T(8,128)(2,1)S(1)} %get-tuple-element.8), channel_id=1, source_target_pairs={{0,3},{1,2},{2,1},{3,0},{4,7},{5,6},{6,5},{7,4},{8,11},{9,10},{10,... | collective-permute-start | bytes 196616 | tf_op jit(solution)/shard_map/ppermute | solution.py:25
  9.8 12.2 %collective-permute-start = (bf16[4,16,512]{2,1,0:T(8,128)(2,1)S(1)}, bf16[4,16,512]{2,1,0:T(8,128)(2,1)S(1)}, u32[]{:S(2)}, u32[]{:S(2)}) collective-permute-start(bf16[4,16,512]{2,1,0:T(8,128)(2,1)S(1)} %get-tuple-element.8), channel_id=1, source_target_pairs={{0,1},{1,0},{2,3},{3,2},{4,5},{5,4},{6,7},{7,6},{8,9},{9,8},{10,11... | collective-permute-start | bytes 196616 | tf_op jit(solution)/shard_map/ppermute | solution.py:25
  20.4 9.0 %collective-permute-start.4 = (bf16[2,4,16,512]{3,2,1,0:T(8,128)(2,1)S(1)}, bf16[2,4,16,512]{3,2,1,0:T(8,128)(2,1)S(1)}, u32[]{:S(2)}, u32[]{:S(2)}) collective-permute-start(bf16[2,4,16,512]{3,2,1,0:T(8,128)(2,1)S(1)} %pad_maximum_fusion.3.rest_1_), channel_id=1, source_target_pairs={{0,16},{4,12},{8,24},{12,4},{16,0},{20,28},{24,8},{28,20},{1,17},{... | collective-permute-start | bytes 393224 | tf_op jit(solution)/shard_map/ppermute | solution.py:36
  22.0 8.4 %collective-permute-start.6 = (bf16[2,4,16,512]{3,2,1,0:T(8,128)(2,1)S(1)}, bf16[2,4,16,512]{3,2,1,0:T(8,128)(2,1)}, u32[]{:S(2)}, u32[]{:S(2)}) collective-permute-start(bf16[2,4,16,512]{3,2,1,0:T(8,128)(2,1)S(1)} %pad_maximum_fusion.3.rest_1_), channel_id=1, source_target_pairs={{0,8},{4,20},{8,0},{12,28},{16,24},{20,4},{24,16},{28,12},{1,9},{5... | collective-permute-start | bytes 393224 | tf_op jit(solution)/shard_map/ppermute | solution.py:36
  24.4 8.1 %collective-permute-start.3 = (bf16[2,4,16,512]{3,2,1,0:T(8,128)(2,1)S(1)}, bf16[2,4,16,512]{3,2,1,0:T(8,128)(2,1)}, u32[]{:S(2)}, u32[]{:S(2)}) collective-permute-start(bf16[2,4,16,512]{3,2,1,0:T(8,128)(2,1)S(1)} %pad_maximum_fusion.2.rest_0_), channel_id=1, source_target_pairs={{0,16},{4,12},{8,24},{12,4},{16,0},{20,28},{24,8},{28,20},{1,17},{... | collective-permute-start | bytes 393224 | tf_op jit(solution)/shard_map/ppermute | solution.py:36
  30.4 7.1 %collective-permute-start.22 = (bf16[2,6,16,512]{3,2,1,0:T(8,128)(2,1)S(1)}, bf16[2,6,16,512]{3,2,1,0:T(8,128)(2,1)S(1)}, u32[]{:S(2)}, u32[]{:S(2)}) collective-permute-start(bf16[2,6,16,512]{3,2,1,0:T(8,128)(2,1)S(1)} %pad_maximum_fusion.1.rest_1_), channel_id=1, source_target_pairs={{0,16},{4,12},{8,24},{12,4},{16,0},{20,28},{24,8},{28,20},{1,17},{... | collective-permute-start | bytes 589832 | tf_op jit(solution)/shard_map/ppermute | solution.py:36
  30.7 11.0 %collective-permute-start.21 = (bf16[2,6,16,512]{3,2,1,0:T(8,128)(2,1)S(1)}, bf16[2,6,16,512]{3,2,1,0:T(8,128)(2,1)S(1)}, u32[]{:S(2)}, u32[]{:S(2)}) collective-permute-start(bf16[2,6,16,512]{3,2,1,0:T(8,128)(2,1)S(1)} %pad_maximum_fusion.rest_0_), channel_id=1, source_target_pairs={{0,16},{4,12},{8,24},{12,4},{16,0},{20,28},{24,8},{28,20},{1,17},{... | collective-permute-start | bytes 589832 | tf_op jit(solution)/shard_map/ppermute | solution.py:36
  32.5 9.6 %collective-permute-start.24 = (bf16[2,6,16,512]{3,2,1,0:T(8,128)(2,1)S(1)}, bf16[2,6,16,512]{3,2,1,0:T(8,128)(2,1)S(1)}, u32[]{:S(2)}, u32[]{:S(2)}) collective-permute-start(bf16[2,6,16,512]{3,2,1,0:T(8,128)(2,1)S(1)} %pad_maximum_fusion.1.rest_1_), channel_id=1, source_target_pairs={{0,8},{4,20},{8,0},{12,28},{16,24},{20,4},{24,16},{28,12},{1,9},{5... | collective-permute-start | bytes 589832 | tf_op jit(solution)/shard_map/ppermute | solution.py:36
  35.3 7.7 %collective-permute-start.23 = (bf16[2,6,16,512]{3,2,1,0:T(8,128)(2,1)S(1)}, bf16[2,6,16,512]{3,2,1,0:T(8,128)(2,1)S(1)}, u32[]{:S(2)}, u32[]{:S(2)}) collective-permute-start(bf16[2,6,16,512]{3,2,1,0:T(8,128)(2,1)S(1)} %pad_maximum_fusion.rest_0_), channel_id=1, source_target_pairs={{0,8},{4,20},{8,0},{12,28},{16,24},{20,4},{24,16},{28,12},{1,9},{5... | collective-permute-start | bytes 589832 | tf_op jit(solution)/shard_map/ppermute | solution.py:36
  36.0 8.3 %collective-permute-start.28 = (bf16[2,6,16,512]{3,2,1,0:T(8,128)(2,1)S(1)}, bf16[2,6,16,512]{3,2,1,0:T(8,128)(2,1)S(1)}, u32[]{:S(2)}, u32[]{:S(2)}) collective-permute-start(bf16[2,6,16,512]{3,2,1,0:T(8,128)(2,1)S(1)} %pad_maximum_fusion.1.rest_1_), channel_id=1, source_target_pairs={{0,4},{4,0},{8,12},{12,8},{1,5},{5,1},{9,13},{13,9},{2,6},{6,2},{1... | collective-permute-start | bytes 589832 | tf_op jit(solution)/shard_map/ppermute | solution.py:25
  37.5 8.4 %collective-permute-start.27 = (bf16[2,6,16,512]{3,2,1,0:T(8,128)(2,1)S(1)}, bf16[2,6,16,512]{3,2,1,0:T(8,128)(2,1)}, u32[]{:S(2)}, u32[]{:S(2)}) collective-permute-start(bf16[2,6,16,512]{3,2,1,0:T(8,128)(2,1)S(1)} %pad_maximum_fusion.rest_0_), channel_id=1, source_target_pairs={{0,4},{4,0},{8,12},{12,8},{1,5},{5,1},{9,13},{13,9},{2,6},{6,2},{1... | collective-permute-start | bytes 589832 | tf_op jit(solution)/shard_map/ppermute | solution.py:25
  43.0 23.4 %collective-permute-start.38 = (bf16[16,128,128]{2,1,0:T(8,128)(2,1)S(1)}, bf16[16,128,128]{2,1,0:T(8,128)(2,1)S(1)}, u32[]{:S(2)}, u32[]{:S(2)}) collective-permute-start(bf16[16,128,128]{2,1,0:T(8,128)(2,1)S(1)} %pad.8.rest_0_), channel_id=1, source_target_pairs={{0,16},{16,0},{1,17},{17,1},{2,18},{18,2},{3,19},{19,3},{4,20},{20... | collective-permute-start | bytes 1572872 | tf_op jit(solution)/shard_map/ppermute | solution.py:25
  45.9 13.4 %collective-permute-start.25 = (bf16[2,6,16,512]{3,2,1,0:T(8,128)(2,1)S(1)}, bf16[2,6,16,512]{3,2,1,0:T(8,128)(2,1)}, u32[]{:S(2)}, u32[]{:S(2)}) collective-permute-start(bf16[2,6,16,512]{3,2,1,0:T(8,128)(2,1)S(1)} %collective-permute-done.21.rest_2_), channel_id=1, source_target_pairs={{0,8},{4,20},{8,0},{12,28},{16,24},{20,4},{24,16},{28,12},{1,9},{5... | collective-permute-start | bytes 589832 | tf_op jit(solution)/shard_map/ppermute | solution.py:36
  47.0 15.2 %collective-permute-start.30 = (bf16[2,6,16,512]{3,2,1,0:T(8,128)(2,1)S(1)}, bf16[2,6,16,512]{3,2,1,0:T(8,128)(2,1)}, u32[]{:S(2)}, u32[]{:S(2)}) collective-permute-start(bf16[2,6,16,512]{3,2,1,0:T(8,128)(2,1)S(1)} %collective-permute-done.22.rest_3_), channel_id=1, source_target_pairs={{0,4},{4,0},{8,12},{12,8},{1,5},{5,1},{9,13},{13,9},{2,6},{6,2},{1... | collective-permute-start | bytes 589832 | tf_op jit(solution)/shard_map/ppermute | solution.py:25
  47.0 15.9 %collective-permute-start.32 = (bf16[2,6,16,512]{3,2,1,0:T(8,128)(2,1)S(1)}, bf16[2,6,16,512]{3,2,1,0:T(8,128)(2,1)}, u32[]{:S(2)}, u32[]{:S(2)}) collective-permute-start(bf16[2,6,16,512]{3,2,1,0:T(8,128)(2,1)S(1)} %collective-permute-done.24.rest_5_), channel_id=1, source_target_pairs={{0,4},{4,0},{8,12},{12,8},{1,5},{5,1},{9,13},{13,9},{2,6},{6,2},{1... | collective-permute-start | bytes 589832 | tf_op jit(solution)/shard_map/ppermute | solution.py:25
  50.6 12.8 %collective-permute-start.29 = (bf16[2,6,16,512]{3,2,1,0:T(8,128)(2,1)S(1)}, bf16[2,6,16,512]{3,2,1,0:T(8,128)(2,1)S(1)}, u32[]{:S(2)}, u32[]{:S(2)}) collective-permute-start(bf16[2,6,16,512]{3,2,1,0:T(8,128)(2,1)S(1)} %collective-permute-done.21.rest_2_), channel_id=1, source_target_pairs={{0,4},{4,0},{8,12},{12,8},{1,5},{5,1},{9,13},{13,9},{2,6},{6,2},{1... | collective-permute-start | bytes 589832 | tf_op jit(solution)/shard_map/ppermute | solution.py:25
  64.1 36.6 %collective-permute-start.39 = (bf16[16,128,128]{2,1,0:T(8,128)(2,1)S(1)}, bf16[16,128,128]{2,1,0:T(8,128)(2,1)S(1)}, u32[]{:S(2)}, u32[]{:S(2)}) collective-permute-start(bf16[16,128,128]{2,1,0:T(8,128)(2,1)S(1)} %pad.8.rest_0_), channel_id=1, source_target_pairs={{0,1},{1,0},{2,3},{3,2},{4,5},{5,4},{6,7},{7,6},{8,9},{9,8},{10,11... | collective-permute-start | bytes 1572872 | tf_op jit(solution)/shard_map/ppermute | solution.py:25
  65.0 19.9 %collective-permute-start.7 = (bf16[2,4,16,512]{3,2,1,0:T(8,128)(2,1)}, bf16[2,4,16,512]{3,2,1,0:T(8,128)(2,1)}, u32[]{:S(2)}, u32[]{:S(2)}) collective-permute-start(bf16[2,4,16,512]{3,2,1,0:T(8,128)(2,1)} %collective-permute-done.3.rest_2_), channel_id=1, source_target_pairs={{0,8},{4,20},{8,0},{12,28},{16,24},{20,4},{24,16},{28,12},{1,9},{5... | collective-permute-start | bytes 393224 | tf_op jit(solution)/shard_map/ppermute | solution.py:36
  66.4 19.1 %collective-permute-start.11 = (bf16[2,4,16,512]{3,2,1,0:T(8,128)(2,1)}, bf16[2,4,16,512]{3,2,1,0:T(8,128)(2,1)}, u32[]{:S(2)}, u32[]{:S(2)}) collective-permute-start(bf16[2,4,16,512]{3,2,1,0:T(8,128)(2,1)} %collective-permute-done.3.rest_2_), channel_id=1, source_target_pairs={{0,4},{4,0},{8,12},{12,8},{1,5},{5,1},{9,13},{13,9},{2,6},{6,2},{1... | collective-permute-start | bytes 393224 | tf_op jit(solution)/shard_map/ppermute | solution.py:25
  67.1 17.8 %collective-permute-start.14 = (bf16[2,4,16,512]{3,2,1,0:T(8,128)(2,1)}, bf16[2,4,16,512]{3,2,1,0:T(8,128)(2,1)}, u32[]{:S(2)}, u32[]{:S(2)}) collective-permute-start(bf16[2,4,16,512]{3,2,1,0:T(8,128)(2,1)} %collective-permute-done.6.rest_5_), channel_id=1, source_target_pairs={{0,4},{4,0},{8,12},{12,8},{1,5},{5,1},{9,13},{13,9},{2,6},{6,2},{1... | collective-permute-start | bytes 393224 | tf_op jit(solution)/shard_map/ppermute | solution.py:25
  68.3 36.0 %collective-permute-start.40 = (bf16[16,128,128]{2,1,0:T(8,128)(2,1)S(1)}, bf16[16,128,128]{2,1,0:T(8,128)(2,1)S(1)}, u32[]{:S(2)}, u32[]{:S(2)}) collective-permute-start(bf16[16,128,128]{2,1,0:T(8,128)(2,1)S(1)} %collective-permute-done.38.rest_1_), channel_id=1, source_target_pairs={{0,1},{1,0},{2,3},{3,2},{4,5},{5,4},{6,7},{7,6},{8,9},{9,8},{10,11... | collective-permute-start | bytes 1572872 | tf_op jit(solution)/shard_map/ppermute | solution.py:25
  (59 other events, 220.9 us)

commit v2 on v1

--- a/solution.py
+++ b/solution.py
@@ -43,35 +43,34 @@
 def gather_weights(own, parts):
     here = (0, 0, 0)
     distances = list(range(lax.axis_size("dp")))
-    received = [own] + [swapped(own, "dp", k) for k in distances[1:]]
+    received = {k: swapped(own, "dp", k) for k in reversed(distances[1:])} | {0: own}
     pieces = []
-    for k in range(0, len(received), 2):
-        pair = received[k : k + 2]
-        origins = [flipped(here, "dp", d) for d in distances[k : k + 2]]
-        pieces.append((jnp.stack(pair), [(o, o) for o in origins]))
+    for k in range(0, len(distances), 2):
+        pair = distances[k : k + 2]
+        origins = [(flipped(here, "dp", d),) * 2 for d in pair]
+        pieces.append((jnp.stack([received[d] for d in pair]), origins))
+
+    def doubled(pieces, send, even, odd):
+        return [
+            (jnp.concatenate([x, send(x)]), origins + [(flipped(e, *even), flipped(o, *odd)) for e, o in origins])
+            for x, origins in pieces
+        ]
+
     section_bits = bits_of(lax.axis_size("section"))
     mixed = parts == 4 and section_bits
     for bit in section_bits[: -1 if mixed else None]:
-        pieces += [
-            (swapped(x, "section", bit), [(flipped(e, "section", bit), flipped(o, "section", bit)) for e, o in origins])
-            for x, origins in pieces
-        ]
+        pieces = doubled(pieces, lambda x, bit=bit: swapped(x, "section", bit), ("section", bit), ("section", bit))
     if mixed:
         bit = section_bits[-1]
-        first = [
-            (swapped_by_parity(x, bit, 2, True), [(flipped(e, "section", bit), flipped(o, "tm", 2)) for e, o in origins])
-            for x, origins in pieces
-        ]
-        both = pieces + first
-        second = [
-            (swapped_by_parity(x, bit, 2, False), [(flipped(e, "tm", 2), flipped(o, "section", bit)) for e, o in origins])
-            for x, origins in both
-        ]
-        pieces = both + second
+        for section_first in (True, False):
+            ways = (("section", bit), ("tm", 2))
+            pieces = doubled(
+                pieces,
+                lambda x, first=section_first: swapped_by_parity(x, bit, 2, first),
+                *(ways if section_first else reversed(ways)),
+            )
     elif parts == 4:
-        pieces += [
-            (swapped(x, "tm", 2), [(flipped(e, "tm", 2), flipped(o, "tm", 2)) for e, o in origins]) for x, origins in pieces
-        ]
+        pieces = doubled(pieces, lambda x: swapped(x, "tm", 2), ("tm", 2), ("tm", 2))
     if parts >= 2:
         pieces += [
             (swapped(x, "tm", 1), [(flipped(o, "tm", 1), flipped(e, "tm", 1)) for e, o in origins]) for x, origins in pieces
@@ -79,14 +78,13 @@
     return [x for x, _ in pieces], [origin for _, origins in pieces for origin in origins]
 
 
-def weight_rows(origins, parts, shard_rows):
-    odd = lax.axis_index("tm") % 2
-    picked = jnp.where(odd == 1, jnp.array([o for _, o in origins]), jnp.array([e for e, _ in origins]))
-    section = lax.axis_index("section") ^ picked[:, 0]
-    stage = lax.axis_index("dp") ^ picked[:, 1]
-    part = (lax.axis_index("tm") % parts) ^ picked[:, 2]
-    shard = section * lax.axis_size("dp") + stage
-    return (shard * shard_rows + part * (shard_rows // parts)).astype(jnp.int32)
+def part_row(origin, parts, shard_rows):
+    even, odd = origin
+    tm = lax.axis_index("tm")
+    distance = [e if e == o else jnp.where(tm % 2 == 1, o, e) for e, o in zip(even, odd, strict=True)]
+    shard = (lax.axis_index("section") ^ distance[0]) * lax.axis_size("dp") + (lax.axis_index("dp") ^ distance[1])
+    part = (tm % parts) ^ distance[2]
+    return pl.multiple_of(shard * shard_rows + part * (shard_rows // parts), ROW_TILE)
 
 
 def layer_norm(values):
@@ -126,29 +124,31 @@
     return gelu(layer_norm(summed)).astype(bf16)
 
 
-def start_assembly(piece_refs, first_rows, tap_slices, weight_refs, sems):
+def start_assembly(piece_refs, origins, parts, shard_rows, tap_slices, weight_refs, sems):
+    first_rows = [part_row(origin, parts, shard_rows) for origin in origins]
     for layer, (low, high) in enumerate(tap_slices):
-        for index, piece in enumerate(piece_refs):
-            slots, rows = piece.shape[0], piece.shape[2]
-            for slot in range(slots):
-                row = pl.multiple_of(first_rows[index * slots + slot], ROW_TILE)
+        part = 0
+        for piece in piece_refs:
+            for slot in range(piece.shape[0]):
                 pltpu.make_async_copy(
                     piece.at[slot, low:high],
-                    weight_refs[layer].at[:, pl.ds(row, rows), :],
+                    weight_refs[layer].at[:, pl.ds(first_rows[part], piece.shape[2]), :],
                     sems.at[layer],
                 ).start()
+                part += 1
 
 
 def wait_assembly(weight_ref, sem):
     pltpu.make_async_copy(weight_ref, weight_ref, sem).wait()
 
 
-def front_kernel(n_pieces, tap_slices, first_rows, scalars, frames, halo, *rest):
+def front_kernel(n_pieces, assembly, lengths, frames, halo, *rest):
     pieces, out = rest[:n_pieces], rest[n_pieces]
     w_a, w_b, x_in, x_mid, sems = rest[n_pieces + 1 :]
-    start_assembly(pieces, first_rows, tap_slices, (w_a, w_b), sems)
-    length, first = scalars[0], scalars[1]
+    start_assembly(pieces, *assembly, (w_a, w_b), sems)
+    length = lengths[0]
     rows, halo_rows = frames.shape[0], halo.shape[0]
+    first = lax.axis_index("tm") * rows
     channels = frames.shape[1]
 
     def masked(values, start):
@@ -164,11 +164,11 @@
     out[...] = strided_conv(x_mid, w_b, out.shape[0])
 
 
-def back_kernel(n_pieces, n_rows, tap_slices, first_rows, scalars, gain, bias, project, project_bias, *rest):
+def back_kernel(n_pieces, n_rows, assembly, lengths, gain, bias, project, project_bias, *rest):
     pieces, row_pieces, out = rest[:n_pieces], rest[n_pieces : n_pieces + n_rows], rest[n_pieces + n_rows]
     w_a, w_b, x_in, x_mid, sems = rest[n_pieces + n_rows + 1 :]
-    start_assembly(pieces, first_rows, tap_slices, (w_a, w_b), sems)
-    length, tm = scalars[0], scalars[2]
+    start_assembly(pieces, *assembly, (w_a, w_b), sems)
+    length, tm = lengths[0], lax.axis_index("tm")
     for index, piece in enumerate(row_pieces):
         rows = piece.shape[0]
         put_rows(x_in, pl.multiple_of((tm ^ index) * rows, ROW_TILE), piece[...])
@@ -185,7 +185,7 @@
     out[:, 0:group] = hidden.astype(bf16)
 
 
-def position_kernel(n_pieces, offsets, hidden, *rest):
+def position_kernel(n_pieces, places, hidden, *rest):
     pieces, out, padded, phases = rest[:n_pieces], rest[n_pieces], rest[n_pieces + 1], rest[n_pieces + 2]
     frames = hidden.shape[0]
     padded[...] = jnp.zeros(padded.shape, f32)
@@ -193,7 +193,9 @@
     taps, width = pieces[0].shape[0], pieces[0].shape[1]
     span = phases.shape[0]
     for index, piece in enumerate(pieces):
-        window = padded[pl.ds(offsets[index], span), :].astype(bf16)
+        shard = (lax.axis_index("section") ^ places[index][0]) * lax.axis_size("dp")
+        shard += lax.axis_index("dp") ^ places[index][1]
+        window = padded[pl.ds(shard * taps, span), :].astype(bf16)
         term = dot_nt(window, piece[...].reshape(taps * width, piece.shape[2]))
         if index == 0:
             phases[...] = term
@@ -211,6 +213,10 @@
     out[...] = jnp.transpose(encoded)[0:group, :].astype(bf16)
 
 
+def layer_taps(counts):
+    return [(sum(counts[:i]), sum(counts[: i + 1])) for i in range(len(counts))]
+
+
 def vmem(count):
     return [pl.BlockSpec(memory_space=pltpu.VMEM)] * count
 
@@ -223,7 +229,7 @@
     return [pl.BlockSpec(memory_space=pl.ANY)] * count
 
 
-LIMIT = pltpu.CompilerParams(vmem_limit_bytes=40 * 1024 * 1024)
+LIMIT = pltpu.CompilerParams(vmem_limit_bytes=16 * 1024 * 1024)
 
 
 def local(
@@ -241,7 +247,7 @@
     position_bias,
 ):
     sections, stages, shares = (lax.axis_size(a) for a in ("section", "dp", "tm"))
-    section, stage, tm = (lax.axis_index(a) for a in ("section", "dp", "tm"))
+    tm = lax.axis_index("tm")
     rows, channels = frames.shape[1:]
     shard_rows = fourth_conv.shape[1]
     parts = max(p for p in (1, 2, 4) if p <= shares and shard_rows % (p * ROW_TILE) == 0)
@@ -255,9 +261,8 @@
 
     halo = lax.ppermute(frames[0, :ROW_TILE], "tm", [(i + 1, i) for i in range(shares - 1)])
     front_pieces, origins = gather_weights(own_part([fourth_conv, fifth_conv]), parts)
-    back_pieces, _ = gather_weights(own_part([sixth_conv, seventh_conv]), parts)
-    first_rows = weight_rows(origins, parts, shard_rows)
-    scalars = jnp.stack([lengths[0], tm * rows, tm]).astype(jnp.int32)
+    back_own, front_pieces[0] = lax.optimization_barrier((own_part([sixth_conv, seventh_conv]), front_pieces[0]))
+    back_pieces, _ = gather_weights(back_own, parts)
 
     group = position_bias.shape[0]
     own_taps = position_weight.shape[1]
@@ -268,18 +273,14 @@
         for bit in bits:
             tap_pieces += [swapped(x, axis, bit) for x in tap_pieces]
             tap_places += [flipped(p, axis, bit) for p in tap_places]
-    offsets = jnp.stack(
-        [((section ^ p[0]) * stages + (stage ^ p[1])) * own_taps for p in tap_places]
-    ).astype(jnp.int32)
-
     taps_of = [w.shape[0] for w in (fourth_conv, fifth_conv, sixth_conv, seventh_conv)]
     n_pieces = len(front_pieces)
     blocks = channels // LANES
     mid_rows = (rows // 2 + 8) // 8 * 8
     y_front = pl.pallas_call(
-        functools.partial(front_kernel, n_pieces, [(0, taps_of[0]), (taps_of[0], taps_of[0] + taps_of[1])]),
+        functools.partial(front_kernel, n_pieces, (origins, parts, shard_rows, layer_taps(taps_of[:2]))),
         out_shape=jax.ShapeDtypeStruct((rows // 4, channels), bf16),
-        in_specs=smem(2) + vmem(2) + unplaced(n_pieces),
+        in_specs=smem(1) + vmem(2) + unplaced(n_pieces),
         out_specs=pl.BlockSpec(memory_space=pltpu.VMEM),
         scratch_shapes=[
             pltpu.VMEM((taps_of[0], channels, channels), bf16),
@@ -289,7 +290,7 @@
             pltpu.SemaphoreType.DMA((2,)),
         ],
         compiler_params=LIMIT,
-    )(first_rows, scalars, frames[0], halo, *front_pieces)
+    )(lengths, frames[0], halo, *front_pieces)
 
     row_pieces = [y_front]
     for bit in reversed(bits_of(shares)):
@@ -302,10 +303,10 @@
 
     hidden = pl.pallas_call(
         functools.partial(
-            back_kernel, n_pieces, len(row_pieces), [(0, taps_of[2]), (taps_of[2], taps_of[2] + taps_of[3])]
+            back_kernel, n_pieces, len(row_pieces), (origins, parts, shard_rows, layer_taps(taps_of[2:]))
         ),
         out_shape=jax.ShapeDtypeStruct((frame_total, LANES), bf16),
-        in_specs=smem(2) + vmem(4) + unplaced(n_pieces) + vmem(len(row_pieces)),
+        in_specs=smem(1) + vmem(4) + unplaced(n_pieces) + vmem(len(row_pieces)),
         out_specs=pl.BlockSpec(memory_space=pltpu.VMEM),
         scratch_shapes=[
             pltpu.VMEM((taps_of[2], channels, channels), bf16),
@@ -316,8 +317,7 @@
         ],
         compiler_params=LIMIT,
     )(
-        first_rows,
-        scalars,
+        lengths,
         norm_gain[None],
         norm_bias[None],
         project_weight.T,
@@ -328,16 +328,16 @@
 
     def partial_position(values, kind):
         return pl.pallas_call(
-            functools.partial(position_kernel, len(tap_pieces)),
+            functools.partial(position_kernel, len(tap_pieces), tap_places),
             out_shape=jax.ShapeDtypeStruct((frame_total, LANES), kind),
-            in_specs=smem(1) + vmem(1 + len(tap_pieces)),
+            in_specs=vmem(1 + len(tap_pieces)),
             out_specs=pl.BlockSpec(memory_space=pltpu.VMEM),
             scratch_shapes=[
                 pltpu.VMEM((frame_total + TAPS, LANES), f32),
                 pltpu.VMEM((frame_total + PHASES, own_taps * LANES), f32),
             ],
             compiler_params=LIMIT,
-        )(offsets, values, *tap_pieces)
+        )(values, *tap_pieces)
 
     far = stages // 2
     partner_hidden = swapped(hidden, "dp", far)

time: 113 us -> 93.5 us (0.83)
  local copies, waits for them, and re-layouts: 22.9 us -> 5.85 us
  starting transfers between devices: 43.9 us -> 38.9 us
  waiting for transfers between devices: 33.2 us -> 36.3 us
    unnamed x80 -> x18, local copies, waits for them, and re-layouts: 20 us -> 1.95 us
    ppermute x30 -> x18, waiting for transfers between devices: 22.3 us -> 26 us  [swapped(): lax.ppermute(x, axis, [(i, i ^ bit) for i in range(lax.axis_size(axis))])]
    ppermute x30 -> x18, starting transfers between devices: 30.5 us -> 27.4 us  [swapped(): lax.ppermute(x, axis, [(i, i ^ bit) for i in range(lax.axis_size(axis))])]
    ppermute x12 -> x8, starting transfers between devices: 12.2 us -> 10.2 us  [swapped_by_parity(): return lax.ppermute(x, ('section', 'tm'), pairs)]
    ppermute x12 -> x8, waiting for transfers between devices: 10.8 us -> 10.2 us  [swapped_by_parity(): return lax.ppermute(x, ('section', 'tm'), pairs)]
  transfers between devices with their start and end apart: 43 -> 27, of which waited for: 11 -> 13; matrix products, arithmetic and copies ran while one was open for 3% -> 5% of each run, Pallas kernels for 7% -> 8%
where the time goes in v2:
time: 93.5 us; the launch traced here: 93.1 us
  starting transfers between devices  38.9 us (42%)
  waiting for transfers between devices  36.3 us (39%)
  Pallas kernels  10.1 us (11%)
  local copies, waits for them, and re-layouts  5.85 us (6%)
  other arithmetic  1.14 us (1%)
    ppermute x18, starting transfers between devices, swapped(): lax.ppermute(x, axis, [(i, i ^ bit) for i in range(lax.axis_size(axis))])  27.4 us
    ppermute x18, waiting for transfers between devices, swapped(): lax.ppermute(x, axis, [(i, i ^ bit) for i in range(lax.axis_size(axis))])  26 us
    ppermute x8, waiting for transfers between devices, swapped_by_parity(): return lax.ppermute(x, ('section', 'tm'), pairs)  10.2 us
    ppermute x8, starting transfers between devices, swapped_by_parity(): return lax.ppermute(x, ('section', 'tm'), pairs)  10.2 us
    pallas_call x1, Pallas kernels, local(): pl.pallas_call(functools.partial(back_kernel, n_pieces, len(row_pieces),...  3.47 us
    pallas_call x1, Pallas kernels, local(): pl.pallas_call(functools.partial(front_kernel, n_pieces, (origins, parts,...  3.46 us
    unnamed x18, local copies, waits for them, and re-layouts  1.95 us
  transfers between devices with their start and end apart: 27, of which 13 were waited for; matrix products, arithmetic and copies ran while one was open for 5% of the time, Pallas kernels for 8%

profile of v2, /device:TPU:0, one launch (start us, length us, event | category | flops | bytes accessed | tf_op | source)
XLA Modules:
  0.0 93.1 jit_solution(11984922812059332143)
XLA Ops:
  0.8 3.1 %collective-permute-start = (bf16[6,16,512]{2,1,0:T(8,128)(2,1)S(1)}, bf16[6,16,512]{2,1,0:T(8,128)(2,1)S(1)}, u32[]{:S(2)}, u32[]{:S(2)}) collective-permute-start(bf16[6,16,512]{2,1,0:T(8,128)(2,1)S(1)} %get-tuple-element.10), channel_id=1, source_target_pairs={{0,1},{1,0},{2,3},{3,2},{4,5},{5,4},{6,7},{7,6},{8,9},{9,8},{10,11... | collective-permute-start | bytes 294920 | tf_op jit(solution)/shard_map/ppermute | solution.py:25
  3.9 2.6 %collective-permute-start.13 = (bf16[6,16,512]{2,1,0:T(8,128)(2,1)S(1)}, bf16[6,16,512]{2,1,0:T(8,128)(2,1)S(1)}, u32[]{:S(2)}, u32[]{:S(2)}) collective-permute-start(bf16[6,16,512]{2,1,0:T(8,128)(2,1)S(1)} %get-tuple-element.10), channel_id=1, source_target_pairs={{0,2},{1,3},{2,0},{3,1},{4,6},{5,7},{6,4},{7,5},{8,10},{9,11},{10,... | collective-permute-start | bytes 294920 | tf_op jit(solution)/shard_map/ppermute | solution.py:25
  6.8 1.8 %collective-permute-start.1 = (bf16[2,6,16,512]{3,2,1,0:T(8,128)(2,1)S(1)}, bf16[2,6,16,512]{3,2,1,0:T(8,128)(2,1)S(1)}, u32[]{:S(2)}, u32[]{:S(2)}) collective-permute-start(bf16[2,6,16,512]{3,2,1,0:T(8,128)(2,1)S(1)} %pad_maximum_fusion.8), channel_id=1, source_target_pairs={{0,16},{4,12},{8,24},{12,4},{16,0},{20,28},{24,8},{28,20},{1,17},{... | collective-permute-start | bytes 589832 | tf_op jit(solution)/shard_map/ppermute | solution.py:36
  8.6 5.8 %collective-permute-done.13 = bf16[6,16,512]{2,1,0:T(8,128)(2,1)S(1)} collective-permute-done((bf16[6,16,512]{2,1,0:T(8,128)(2,1)S(1)}, bf16[6,16,512]{2,1,0:T(8,128)(2,1)S(1)}, u32[]{:S(2)}, u32[]{:S(2)}) %collective-permute-start.13) | collective-permute-done | bytes 98336 | tf_op jit(solution)/shard_map/ppermute | solution.py:25
  14.4 1.6 %collective-permute-start.15 = (bf16[2,6,16,512]{3,2,1,0:T(8,128)(2,1)S(1)}, bf16[2,6,16,512]{3,2,1,0:T(8,128)(2,1)S(1)}, u32[]{:S(2)}, u32[]{:S(2)}) collective-permute-start(bf16[2,6,16,512]{3,2,1,0:T(8,128)(2,1)S(1)} %pad_maximum_fusion.9), channel_id=1, source_target_pairs={{0,16},{4,12},{8,24},{12,4},{16,0},{20,28},{24,8},{28,20},{1,17},{... | collective-permute-start | bytes 589832 | tf_op jit(solution)/shard_map/ppermute | solution.py:36
  16.0 1.6 %collective-permute-start.2 = (bf16[4,6,16,512]{3,2,1,0:T(8,128)(2,1)S(1)}, bf16[4,6,16,512]{3,2,1,0:T(8,128)(2,1)S(1)}, u32[]{:S(2)}, u32[]{:S(2)}) collective-permute-start(bf16[4,6,16,512]{3,2,1,0:T(8,128)(2,1)S(1)} %pad_maximum_fusion.4), channel_id=1, source_target_pairs={{0,8},{4,20},{8,0},{12,28},{16,24},{20,4},{24,16},{28,12},{1,9},{5... | collective-permute-start | bytes 1179656 | tf_op jit(solution)/shard_map/ppermute | solution.py:36
  18.4 3.9 %collective-permute-done.15 = bf16[2,6,16,512]{3,2,1,0:T(8,128)(2,1)S(1)} collective-permute-done((bf16[2,6,16,512]{3,2,1,0:T(8,128)(2,1)S(1)}, bf16[2,6,16,512]{3,2,1,0:T(8,128)(2,1)S(1)}, u32[]{:S(2)}, u32[]{:S(2)}) %collective-permute-start.15) | collective-permute-done | bytes 196640 | tf_op jit(solution)/shard_map/ppermute | solution.py:36
  22.3 1.6 %collective-permute-start.16 = (bf16[4,6,16,512]{3,2,1,0:T(8,128)(2,1)S(1)}, bf16[4,6,16,512]{3,2,1,0:T(8,128)(2,1)S(1)}, u32[]{:S(2)}, u32[]{:S(2)}) collective-permute-start(bf16[4,6,16,512]{3,2,1,0:T(8,128)(2,1)S(1)} %pad_maximum_fusion.5), channel_id=1, source_target_pairs={{0,8},{4,20},{8,0},{12,28},{16,24},{20,4},{24,16},{28,12},{1,9},{5... | collective-permute-start | bytes 1179656 | tf_op jit(solution)/shard_map/ppermute | solution.py:36
  24.0 2.7 %collective-permute-start.6 = (bf16[4,16,512]{2,1,0:T(8,128)(2,1)S(1)}, bf16[4,16,512]{2,1,0:T(8,128)(2,1)S(1)}, u32[]{:S(2)}, u32[]{:S(2)}) collective-permute-start(bf16[4,16,512]{2,1,0:T(8,128)(2,1)S(1)} %pad_maximum_fusion.13), channel_id=1, source_target_pairs={{0,2},{1,3},{2,0},{3,1},{4,6},{5,7},{6,4},{7,5},{8,10},{9,11},{10,... | collective-permute-start | bytes 196616 | tf_op jit(solution)/shard_map/ppermute | solution.py:25
  28.1 3.5 %collective-permute-done.6 = bf16[4,16,512]{2,1,0:T(8,128)(2,1)S(1)} collective-permute-done((bf16[4,16,512]{2,1,0:T(8,128)(2,1)S(1)}, bf16[4,16,512]{2,1,0:T(8,128)(2,1)S(1)}, u32[]{:S(2)}, u32[]{:S(2)}) %collective-permute-start.6) | collective-permute-done | bytes 65568 | tf_op jit(solution)/shard_map/ppermute | solution.py:25
  33.0 1.5 %collective-permute-start.8 = (bf16[2,4,16,512]{3,2,1,0:T(8,128)(2,1)S(1)}, bf16[2,4,16,512]{3,2,1,0:T(8,128)(2,1)S(1)}, u32[]{:S(2)}, u32[]{:S(2)}) collective-permute-start(bf16[2,4,16,512]{3,2,1,0:T(8,128)(2,1)S(1)} %pad_maximum_fusion.11), channel_id=1, source_target_pairs={{0,16},{4,12},{8,24},{12,4},{16,0},{20,28},{24,8},{28,20},{1,17},{... | collective-permute-start | bytes 393224 | tf_op jit(solution)/shard_map/ppermute | solution.py:36
  35.9 1.7 %reshape_squeeze.3 = bf16[16,120,120]{2,1,0:T(8,128)(2,1)S(1)} reshape(bf16[1,16,14400]{2,1,0:T(8,128)(2,1)} %param.22) | data formatting | bytes 921600 | tf_op jit(solution)/shard_map/reshape;squeeze | solution.py:269
  37.7 1.5 %collective-permute-start.22 = (bf16[16,128,128]{2,1,0:T(8,128)(2,1)S(1)}, bf16[16,128,128]{2,1,0:T(8,128)(2,1)S(1)}, u32[]{:S(2)}, u32[]{:S(2)}) collective-permute-start(bf16[16,128,128]{2,1,0:T(8,128)(2,1)S(1)} %pad.8.rest_0_), channel_id=1, source_target_pairs={{0,16},{16,0},{1,17},{17,1},{2,18},{18,2},{3,19},{19,3},{4,20},{20... | collective-permute-start | bytes 1572872 | tf_op jit(solution)/shard_map/ppermute | solution.py:25
  41.5 4.2 %collective-permute-done.9 = bf16[4,4,16,512]{3,2,1,0:T(8,128)(2,1)S(1)} collective-permute-done((bf16[4,4,16,512]{3,2,1,0:T(8,128)(2,1)S(1)}, bf16[4,4,16,512]{3,2,1,0:T(8,128)(2,1)S(1)}, u32[]{:S(2)}, u32[]{:S(2)}) %collective-permute-start.9) | collective-permute-done | bytes 262176 | tf_op jit(solution)/shard_map/ppermute | solution.py:36
  47.1 1.5 %collective-permute-done.5 = bf16[4,4,16,512]{3,2,1,0:T(8,128)(2,1)S(1)} collective-permute-done((bf16[4,4,16,512]{3,2,1,0:T(8,128)(2,1)S(1)}, bf16[4,4,16,512]{3,2,1,0:T(8,128)(2,1)S(1)}, u32[]{:S(2)}, u32[]{:S(2)}) %collective-permute-start.5) | collective-permute-done | bytes 262176 | tf_op jit(solution)/shard_map/ppermute | solution.py:36
  48.5 8.7 %collective-permute-start.11 = (bf16[8,4,16,512]{3,2,1,0:T(8,128)(2,1)S(1)}, bf16[8,4,16,512]{3,2,1,0:T(8,128)(2,1)S(1)}, u32[]{:S(2)}, u32[]{:S(2)}) collective-permute-start(bf16[8,4,16,512]{3,2,1,0:T(8,128)(2,1)S(1)} %pad_maximum_fusion.3.rest_1_), channel_id=1, source_target_pairs={{0,4},{4,0},{8,12},{12,8},{1,5},{5,1},{9,13},{13,9},{2,6},{6,2},{1... | collective-permute-start | bytes 1572872 | tf_op jit(solution)/shard_map/ppermute | solution.py:25
  57.3 2.2 %collective-permute-start.10 = (bf16[8,4,16,512]{3,2,1,0:T(8,128)(2,1)S(1)}, bf16[8,4,16,512]{3,2,1,0:T(8,128)(2,1)S(1)}, u32[]{:S(2)}, u32[]{:S(2)}) collective-permute-start(bf16[8,4,16,512]{3,2,1,0:T(8,128)(2,1)S(1)} %pad_maximum_fusion.2.rest_0_), channel_id=1, source_target_pairs={{0,4},{4,0},{8,12},{12,8},{1,5},{5,1},{9,13},{13,9},{2,6},{6,2},{1... | collective-permute-start | bytes 1572872 | tf_op jit(solution)/shard_map/ppermute | solution.py:25
  60.1 1.4 %collective-permute-start.24 = (bf16[16,128,128]{2,1,0:T(8,128)(2,1)S(1)}, bf16[16,128,128]{2,1,0:T(8,128)(2,1)S(1)}, u32[]{:S(2)}, u32[]{:S(2)}) collective-permute-start(bf16[16,128,128]{2,1,0:T(8,128)(2,1)S(1)} %collective-permute-done.22.rest_1_), channel_id=1, source_target_pairs={{0,1},{1,0},{2,3},{3,2},{4,5},{5,4},{6,7},{7,6},{8,9},{9,8},{10,11... | collective-permute-start | bytes 1572872 | tf_op jit(solution)/shard_map/ppermute | solution.py:25
  62.2 3.5 %shard_map.118.rest_4_ = bf16[128,512]{1,0:T(8,128)(2,1)S(1)} custom-call(s32[1]{0:T(128)S(6)} %copy.13.lengths, bf16[512,512]{1,0:T(8,128)(2,1)S(1)} %bitcast.18, bf16[16,512]{1,0:T(8,128)(2,1)S(1)} %collective-permute-done.12.halo, bf16[8,6,16,512]{3,2,1,0:T(8,128)(2,1)S(1)} %pad_maximum_fusion.rest_0_, ...), custom_call_target="tpu_custom_call" | custom-call | tf_op jit(solution)/shard_map/pallas_call | solution.py:280
  65.7 5.0 %collective-permute-done.20.rest_6_ = bf16[128,512]{1,0:T(8,128)(2,1)S(1)} collective-permute-done((bf16[128,512]{1,0:T(8,128)(2,1)S(1)}, bf16[128,512]{1,0:T(8,128)(2,1)S(1)}, u32[]{:S(2)}, u32[]{:S(2)}) %collective-permute-start.20) | collective-permute-done | bytes 131104 | tf_op jit(solution)/shard_map/ppermute | solution.py:25
  74.1 3.5 %shard_map.119.hidden = bf16[128,128]{1,0:T(8,128)(2,1)S(1)} custom-call(s32[1]{0:T(128)S(6)} %copy.13.lengths, f32[1,512]{1,0:T(1,128)S(1)} %bitcast.20, f32[1,512]{1,0:T(1,128)S(1)} %bitcast.21, bf16[120,512]{1,0:T(8,128)(2,1)S(1)} %bitcast.19, bf16[1,120]{1,0:T(2,128)(2,1)S(1)} %copy-done.6, bf16[8,4,16,512]{3,2,1,0:T(8,128)(2,1)S(1)} %pad_maximum_fusion.2.rest_0_, ...), custom_call_target="tpu_custom_call" | custom-call | tf_op jit(solution)/shard_map/pallas_call | solution.py:304
  79.0 6.3 %collective-permute-done.24.rest_3_ = bf16[16,128,128]{2,1,0:T(8,128)(2,1)S(1)} collective-permute-done((bf16[16,128,128]{2,1,0:T(8,128)(2,1)S(1)}, bf16[16,128,128]{2,1,0:T(8,128)(2,1)S(1)}, u32[]{:S(2)}, u32[]{:S(2)}) %collective-permute-start.24) | collective-permute-done | bytes 524320 | tf_op jit(solution)/shard_map/ppermute | solution.py:25
  86.0 1.6 %collective-permute-start.26 = (bf16[128,128]{1,0:T(8,128)(2,1)S(1)}, bf16[128,128]{1,0:T(8,128)(2,1)S(1)}, u32[]{:S(2)}, u32[]{:S(2)}) collective-permute-start(bf16[128,128]{1,0:T(8,128)(2,1)S(1)} %shard_map.121), channel_id=1, source_target_pairs={{0,2},{1,3},{2,0},{3,1},{4,6},{5,7},{6,4},{7,5},{8,10},{9,11},{10,... | collective-permute-start | bytes 98312 | tf_op jit(solution)/shard_map/ppermute | solution.py:25
  91.5 1.6 %shard_map.122 = bf16[120,128]{1,0:T(8,128)(2,1)} custom-call(bf16[128,128]{1,0:T(8,128)(2,1)} %copy-done.1, f32[128,128]{1,0:T(8,128)} %copy-done.2, bf16[128,128]{1,0:T(8,128)(2,1)} %copy-done.7, f32[1,128]{1,0:T(1,128)} %pad_bitcast_fusion.bias), custom_call_target="tpu_custom_call" | custom-call | tf_op jit(solution)/shard_map/pallas_call | solution.py:347
  (73 shorter events, 20.1 us)
Async XLA Ops:
  0.8 5.9 %collective-permute-start = (bf16[6,16,512]{2,1,0:T(8,128)(2,1)S(1)}, bf16[6,16,512]{2,1,0:T(8,128)(2,1)S(1)}, u32[]{:S(2)}, u32[]{:S(2)}) collective-permute-start(bf16[6,16,512]{2,1,0:T(8,128)(2,1)S(1)} %get-tuple-element.10), channel_id=1, source_target_pairs={{0,1},{1,0},{2,3},{3,2},{4,5},{5,4},{6,7},{7,6},{8,9},{9,8},{10,11... | collective-permute-start | bytes 294920 | tf_op jit(solution)/shard_map/ppermute | solution.py:25
  3.9 10.4 %collective-permute-start.13 = (bf16[6,16,512]{2,1,0:T(8,128)(2,1)S(1)}, bf16[6,16,512]{2,1,0:T(8,128)(2,1)S(1)}, u32[]{:S(2)}, u32[]{:S(2)}) collective-permute-start(bf16[6,16,512]{2,1,0:T(8,128)(2,1)S(1)} %get-tuple-element.10), channel_id=1, source_target_pairs={{0,2},{1,3},{2,0},{3,1},{4,6},{5,7},{6,4},{7,5},{8,10},{9,11},{10,... | collective-permute-start | bytes 294920 | tf_op jit(solution)/shard_map/ppermute | solution.py:25
  6.5 7.8 %collective-permute-start.14 = (bf16[6,16,512]{2,1,0:T(8,128)(2,1)S(1)}, bf16[6,16,512]{2,1,0:T(8,128)(2,1)S(1)}, u32[]{:S(2)}, u32[]{:S(2)}) collective-permute-start(bf16[6,16,512]{2,1,0:T(8,128)(2,1)S(1)} %get-tuple-element.10), channel_id=1, source_target_pairs={{0,3},{1,2},{2,1},{3,0},{4,7},{5,6},{6,5},{7,4},{8,11},{9,10},{10,... | collective-permute-start | bytes 294920 | tf_op jit(solution)/shard_map/ppermute | solution.py:25
  6.8 9.2 %collective-permute-start.1 = (bf16[2,6,16,512]{3,2,1,0:T(8,128)(2,1)S(1)}, bf16[2,6,16,512]{3,2,1,0:T(8,128)(2,1)S(1)}, u32[]{:S(2)}, u32[]{:S(2)}) collective-permute-start(bf16[2,6,16,512]{3,2,1,0:T(8,128)(2,1)S(1)} %pad_maximum_fusion.8), channel_id=1, source_target_pairs={{0,16},{4,12},{8,24},{12,4},{16,0},{20,28},{24,8},{28,20},{1,17},{... | collective-permute-start | bytes 589832 | tf_op jit(solution)/shard_map/ppermute | solution.py:36
  14.4 7.9 %collective-permute-start.15 = (bf16[2,6,16,512]{3,2,1,0:T(8,128)(2,1)S(1)}, bf16[2,6,16,512]{3,2,1,0:T(8,128)(2,1)S(1)}, u32[]{:S(2)}, u32[]{:S(2)}) collective-permute-start(bf16[2,6,16,512]{3,2,1,0:T(8,128)(2,1)S(1)} %pad_maximum_fusion.9), channel_id=1, source_target_pairs={{0,16},{4,12},{8,24},{12,4},{16,0},{20,28},{24,8},{28,20},{1,17},{... | collective-permute-start | bytes 589832 | tf_op jit(solution)/shard_map/ppermute | solution.py:36
  16.0 7.9 %collective-permute-start.2 = (bf16[4,6,16,512]{3,2,1,0:T(8,128)(2,1)S(1)}, bf16[4,6,16,512]{3,2,1,0:T(8,128)(2,1)S(1)}, u32[]{:S(2)}, u32[]{:S(2)}) collective-permute-start(bf16[4,6,16,512]{3,2,1,0:T(8,128)(2,1)S(1)} %pad_maximum_fusion.4), channel_id=1, source_target_pairs={{0,8},{4,20},{8,0},{12,28},{16,24},{20,4},{24,16},{28,12},{1,9},{5... | collective-permute-start | bytes 1179656 | tf_op jit(solution)/shard_map/ppermute | solution.py:36
  22.3 12.1 %collective-permute-start.16 = (bf16[4,6,16,512]{3,2,1,0:T(8,128)(2,1)S(1)}, bf16[4,6,16,512]{3,2,1,0:T(8,128)(2,1)S(1)}, u32[]{:S(2)}, u32[]{:S(2)}) collective-permute-start(bf16[4,6,16,512]{3,2,1,0:T(8,128)(2,1)S(1)} %pad_maximum_fusion.5), channel_id=1, source_target_pairs={{0,8},{4,20},{8,0},{12,28},{16,24},{20,4},{24,16},{28,12},{1,9},{5... | collective-permute-start | bytes 1179656 | tf_op jit(solution)/shard_map/ppermute | solution.py:36
  24.0 7.6 %collective-permute-start.6 = (bf16[4,16,512]{2,1,0:T(8,128)(2,1)S(1)}, bf16[4,16,512]{2,1,0:T(8,128)(2,1)S(1)}, u32[]{:S(2)}, u32[]{:S(2)}) collective-permute-start(bf16[4,16,512]{2,1,0:T(8,128)(2,1)S(1)} %pad_maximum_fusion.13), channel_id=1, source_target_pairs={{0,2},{1,3},{2,0},{3,1},{4,6},{5,7},{6,4},{7,5},{8,10},{9,11},{10,... | collective-permute-start | bytes 196616 | tf_op jit(solution)/shard_map/ppermute | solution.py:25
  26.7 6.2 %collective-permute-start.7 = (bf16[4,16,512]{2,1,0:T(8,128)(2,1)S(1)}, bf16[4,16,512]{2,1,0:T(8,128)(2,1)S(1)}, u32[]{:S(2)}, u32[]{:S(2)}) collective-permute-start(bf16[4,16,512]{2,1,0:T(8,128)(2,1)S(1)} %pad_maximum_fusion.13), channel_id=1, source_target_pairs={{0,3},{1,2},{2,1},{3,0},{4,7},{5,6},{6,5},{7,4},{8,11},{9,10},{10,... | collective-permute-start | bytes 196616 | tf_op jit(solution)/shard_map/ppermute | solution.py:25
  28.1 6.6 %collective-permute-start.3 = (bf16[4,16,512]{2,1,0:T(8,128)(2,1)S(1)}, bf16[4,16,512]{2,1,0:T(8,128)(2,1)S(1)}, u32[]{:S(2)}, u32[]{:S(2)}) collective-permute-start(bf16[4,16,512]{2,1,0:T(8,128)(2,1)S(1)} %pad_maximum_fusion.13), channel_id=1, source_target_pairs={{0,1},{1,0},{2,3},{3,2},{4,5},{5,4},{6,7},{7,6},{8,9},{9,8},{10,11... | collective-permute-start | bytes 196616 | tf_op jit(solution)/shard_map/ppermute | solution.py:25
  33.0 6.3 %collective-permute-start.8 = (bf16[2,4,16,512]{3,2,1,0:T(8,128)(2,1)S(1)}, bf16[2,4,16,512]{3,2,1,0:T(8,128)(2,1)S(1)}, u32[]{:S(2)}, u32[]{:S(2)}) collective-permute-start(bf16[2,4,16,512]{3,2,1,0:T(8,128)(2,1)S(1)} %pad_maximum_fusion.11), channel_id=1, source_target_pairs={{0,16},{4,12},{8,24},{12,4},{16,0},{20,28},{24,8},{28,20},{1,17},{... | collective-permute-start | bytes 393224 | tf_op jit(solution)/shard_map/ppermute | solution.py:36
  34.6 25.6 %collective-permute-start.18 = (bf16[8,6,16,512]{3,2,1,0:T(8,128)(2,1)S(1)}, bf16[8,6,16,512]{3,2,1,0:T(8,128)(2,1)S(1)}, u32[]{:S(2)}, u32[]{:S(2)}) collective-permute-start(bf16[8,6,16,512]{3,2,1,0:T(8,128)(2,1)S(1)} %pad_maximum_fusion.1.rest_1_), channel_id=1, source_target_pairs={{0,4},{4,0},{8,12},{12,8},{1,5},{5,1},{9,13},{13,9},{2,6},{6,2},{1... | collective-permute-start | bytes 2359304 | tf_op jit(solution)/shard_map/ppermute | solution.py:25
  35.3 5.2 %collective-permute-start.4 = (bf16[2,4,16,512]{3,2,1,0:T(8,128)(2,1)}, bf16[2,4,16,512]{3,2,1,0:T(8,128)(2,1)S(1)}, u32[]{:S(2)}, u32[]{:S(2)}) collective-permute-start(bf16[2,4,16,512]{3,2,1,0:T(8,128)(2,1)} %pad_maximum_fusion.10), channel_id=1, source_target_pairs={{0,16},{4,12},{8,24},{12,4},{16,0},{20,28},{24,8},{28,20},{1,17},{... | collective-permute-start | bytes 393224 | tf_op jit(solution)/shard_map/ppermute | solution.py:36
  37.7 21.7 %collective-permute-start.22 = (bf16[16,128,128]{2,1,0:T(8,128)(2,1)S(1)}, bf16[16,128,128]{2,1,0:T(8,128)(2,1)S(1)}, u32[]{:S(2)}, u32[]{:S(2)}) collective-permute-start(bf16[16,128,128]{2,1,0:T(8,128)(2,1)S(1)} %pad.8.rest_0_), channel_id=1, source_target_pairs={{0,16},{16,0},{1,17},{17,1},{2,18},{18,2},{3,19},{19,3},{4,20},{20... | collective-permute-start | bytes 1572872 | tf_op jit(solution)/shard_map/ppermute | solution.py:25
  39.2 22.9 %collective-permute-start.17 = (bf16[8,6,16,512]{3,2,1,0:T(8,128)(2,1)S(1)}, bf16[8,6,16,512]{3,2,1,0:T(8,128)(2,1)S(1)}, u32[]{:S(2)}, u32[]{:S(2)}) collective-permute-start(bf16[8,6,16,512]{3,2,1,0:T(8,128)(2,1)S(1)} %pad_maximum_fusion.rest_0_), channel_id=1, source_target_pairs={{0,4},{4,0},{8,12},{12,8},{1,5},{5,1},{9,13},{13,9},{2,6},{6,2},{1... | collective-permute-start | bytes 2359304 | tf_op jit(solution)/shard_map/ppermute | solution.py:25
  39.3 6.4 %collective-permute-start.9 = (bf16[4,4,16,512]{3,2,1,0:T(8,128)(2,1)S(1)}, bf16[4,4,16,512]{3,2,1,0:T(8,128)(2,1)S(1)}, u32[]{:S(2)}, u32[]{:S(2)}) collective-permute-start(bf16[4,4,16,512]{3,2,1,0:T(8,128)(2,1)S(1)} %pad_maximum_fusion.7), channel_id=1, source_target_pairs={{0,8},{4,20},{8,0},{12,28},{16,24},{20,4},{24,16},{28,12},{1,9},{5... | collective-permute-start | bytes 786440 | tf_op jit(solution)/shard_map/ppermute | solution.py:36
  40.5 8.0 %collective-permute-start.5 = (bf16[4,4,16,512]{3,2,1,0:T(8,128)(2,1)S(1)}, bf16[4,4,16,512]{3,2,1,0:T(8,128)(2,1)S(1)}, u32[]{:S(2)}, u32[]{:S(2)}) collective-permute-start(bf16[4,4,16,512]{3,2,1,0:T(8,128)(2,1)S(1)} %pad_maximum_fusion.6), channel_id=1, source_target_pairs={{0,8},{4,20},{8,0},{12,28},{16,24},{20,4},{24,16},{28,12},{1,9},{5... | collective-permute-start | bytes 786440 | tf_op jit(solution)/shard_map/ppermute | solution.py:36
  45.7 11.6 %collective-permute-start.12 = (bf16[16,512]{1,0:T(8,128)(2,1)S(1)}, bf16[16,512]{1,0:T(8,128)(2,1)S(1)}, u32[]{:S(2)}, u32[]{:S(2)}) collective-permute-start(bf16[16,512]{1,0:T(8,128)(2,1)S(1)} %slice_bitcast_fusion), channel_id=1, source_target_pairs={{4,0},{8,4},{12,8},{5,1},{9,5},{13,9},{6,2},{10,6},{14,10},{7,3},{... | collective-permute-start | bytes 49160 | tf_op jit(solution)/shard_map/ppermute | solution.py:262
  48.5 23.7 %collective-permute-start.11 = (bf16[8,4,16,512]{3,2,1,0:T(8,128)(2,1)S(1)}, bf16[8,4,16,512]{3,2,1,0:T(8,128)(2,1)S(1)}, u32[]{:S(2)}, u32[]{:S(2)}) collective-permute-start(bf16[8,4,16,512]{3,2,1,0:T(8,128)(2,1)S(1)} %pad_maximum_fusion.3.rest_1_), channel_id=1, source_target_pairs={{0,4},{4,0},{8,12},{12,8},{1,5},{5,1},{9,13},{13,9},{2,6},{6,2},{1... | collective-permute-start | bytes 1572872 | tf_op jit(solution)/shard_map/ppermute | solution.py:25
  57.3 14.9 %collective-permute-start.10 = (bf16[8,4,16,512]{3,2,1,0:T(8,128)(2,1)S(1)}, bf16[8,4,16,512]{3,2,1,0:T(8,128)(2,1)S(1)}, u32[]{:S(2)}, u32[]{:S(2)}) collective-permute-start(bf16[8,4,16,512]{3,2,1,0:T(8,128)(2,1)S(1)} %pad_maximum_fusion.2.rest_0_), channel_id=1, source_target_pairs={{0,4},{4,0},{8,12},{12,8},{1,5},{5,1},{9,13},{13,9},{2,6},{6,2},{1... | collective-permute-start | bytes 1572872 | tf_op jit(solution)/shard_map/ppermute | solution.py:25
  59.5 19.5 %collective-permute-start.23 = (bf16[16,128,128]{2,1,0:T(8,128)(2,1)S(1)}, bf16[16,128,128]{2,1,0:T(8,128)(2,1)S(1)}, u32[]{:S(2)}, u32[]{:S(2)}) collective-permute-start(bf16[16,128,128]{2,1,0:T(8,128)(2,1)S(1)} %pad.8.rest_0_), channel_id=1, source_target_pairs={{0,1},{1,0},{2,3},{3,2},{4,5},{5,4},{6,7},{7,6},{8,9},{9,8},{10,11... | collective-permute-start | bytes 1572872 | tf_op jit(solution)/shard_map/ppermute | solution.py:25
  60.1 25.1 %collective-permute-start.24 = (bf16[16,128,128]{2,1,0:T(8,128)(2,1)S(1)}, bf16[16,128,128]{2,1,0:T(8,128)(2,1)S(1)}, u32[]{:S(2)}, u32[]{:S(2)}) collective-permute-start(bf16[16,128,128]{2,1,0:T(8,128)(2,1)S(1)} %collective-permute-done.22.rest_1_), channel_id=1, source_target_pairs={{0,1},{1,0},{2,3},{3,2},{4,5},{5,4},{6,7},{7,6},{8,9},{9,8},{10,11... | collective-permute-start | bytes 1572872 | tf_op jit(solution)/shard_map/ppermute | solution.py:25
  65.7 5.0 %collective-permute-start.20 = (bf16[128,512]{1,0:T(8,128)(2,1)S(1)}, bf16[128,512]{1,0:T(8,128)(2,1)S(1)}, u32[]{:S(2)}, u32[]{:S(2)}) collective-permute-start(bf16[128,512]{1,0:T(8,128)(2,1)S(1)} %shard_map.118.rest_4_), channel_id=1, source_target_pairs={{0,8},{4,12},{8,0},{12,4},{1,9},{5,13},{9,1},{13,5},{2,10},{6,14},... | collective-permute-start | bytes 393224 | tf_op jit(solution)/shard_map/ppermute | solution.py:25
  77.6 7.6 %collective-permute-start.25 = (bf16[128,128]{1,0:T(8,128)(2,1)S(1)}, bf16[128,128]{1,0:T(8,128)(2,1)S(1)}, u32[]{:S(2)}, u32[]{:S(2)}) collective-permute-start(bf16[128,128]{1,0:T(8,128)(2,1)S(1)} %shard_map.119.hidden), channel_id=1, source_target_pairs={{0,2},{1,3},{2,0},{3,1},{4,6},{5,7},{6,4},{7,5},{8,10},{9,11},{10,... | collective-permute-start | bytes 98312 | tf_op jit(solution)/shard_map/ppermute | solution.py:25
  (12 other events, 46.5 us)

commit v3 on v2

v3 whole, which is shorter than its diff:
```python
import functools

import jax
import jax.numpy as jnp
from jax import lax
from jax.experimental import pallas as pl
from jax.experimental.pallas import tpu as pltpu
from jax.sharding import PartitionSpec as P

TAPS = 128
ROW_TILE = 16
LANES = 128
PHASES = 16
SHARDED = ("section", "dp")
eps_norm = 1e-05
f32 = jnp.float32
bf16 = jnp.bfloat16


def bits_of(size):
    return [1 << b for b in range(size.bit_length() - 1)]


def swapped(x, axis, bit):
    return lax.ppermute(x, axis, [(i, i ^ bit) for i in range(lax.axis_size(axis))])


def swapped_by_parity(x, section_bit, tm_bit, section_first):
    sections, shares = lax.axis_size("section"), lax.axis_size("tm")
    pairs = []
    for s in range(sections):
        for t in range(shares):
            over_section = (t % 2 == 0) == section_first
            to = (s ^ section_bit, t) if over_section else (s, t ^ tm_bit)
            pairs.append((s * shares + t, to[0] * shares + to[1]))
    return lax.ppermute(x, ("section", "tm"), pairs)


def flipped(where, axis, bit):
    return tuple(w ^ (bit if name == axis else 0) for w, name in zip(where, ("section", "dp", "tm"), strict=True))


def after(x, *others):
    return lax.optimization_barrier((x, *others))[0]


def paired(received):
    odd = lax.axis_index("dp") % 2 == 1
    pieces = []
    for first in range(0, len(received), 2):
        one, other = received[first : first + 2]
        pair = jnp.where(odd, jnp.stack([other, one]), jnp.stack([one, other]))
        pieces.append((pair, [((0, first, 0),) * 2]))
    return pieces


def gated(pieces, *others):
    return pieces[:-1] + [(after(pieces[-1][0], *others), pieces[-1][1])]


def wide_steps(parts):
    bits = bits_of(lax.axis_size("section"))
    mixed = parts == 4 and len(bits) > 0
    steps = []
    for bit in bits[: -1 if mixed else None]:
        steps.append((lambda x, bit=bit: swapped(x, "section", bit), ("section", bit), ("section", bit)))
    if mixed:
        ways = (("section", bits[-1]), ("tm", 2))
        steps.append((lambda x: swapped_by_parity(x, bits[-1], 2, True), *ways))
        steps.append((lambda x: swapped_by_parity(x, bits[-1], 2, False), *reversed(ways)))
    elif parts == 4:
        steps.append((lambda x: swapped(x, "tm", 2), ("tm", 2), ("tm", 2)))
    return steps


def doubled(pieces, step):
    send, even, odd = step
    return [
        (jnp.concatenate([x, send(x)]), origins + [(flipped(e, *even), flipped(o, *odd)) for e, o in origins])
        for x, origins in pieces
    ]


def sent(piece, step):
    (x, origins), (send, even, odd) = piece, step
    return send(x), [(flipped(e, *even), flipped(o, *odd)) for e, o in origins]


def joined(*pieces):
    return jnp.concatenate([x for x, _ in pieces]), [origin for _, origins in pieces for origin in origins]


def with_cores(pieces, parts):
    if parts >= 2:
        pieces = pieces + [
            (swapped(x, "tm", 1), [(flipped(o, "tm", 1), flipped(e, "tm", 1)) for e, o in origins]) for x, origins in pieces
        ]
    return [x for x, _ in pieces], [origin for _, origins in pieces for origin in origins]


def layer_norm(values):
    average = jnp.mean(values, axis=-1, keepdims=True)
    centred = values - average
    spread = jnp.mean(centred * centred, axis=-1, keepdims=True)
    return centred * lax.rsqrt(spread + eps_norm)


def gelu(values):
    return 0.5 * values * (1.0 + lax.erf(values * (0.5**0.5)))


def dot(a, b):
    return jnp.dot(a, b, preferred_element_type=f32)


def dot_nt(a, b):
    return lax.dot_general(a, b, (((1,), (1,)), ((), ())), preferred_element_type=f32)


def put_rows(rows_ref, start, values):
    values = values.astype(f32)
    for block in range(rows_ref.shape[0]):
        rows_ref[block, pl.ds(start, values.shape[0]), :] = values[:, block * LANES : (block + 1) * LANES]


def strided_conv(rows_ref, weights_ref, taps, out_rows):
    channels = weights_ref.shape[3]
    summed = None
    for tap in range(taps[1] - taps[0]):
        picked = jnp.concatenate(
            [rows_ref[block, pl.ds(tap, out_rows, stride=2), :].astype(bf16) for block in range(rows_ref.shape[0])],
            axis=1,
        )
        term = dot(picked, weights_ref[:, taps[0] + tap].reshape(channels, channels))
        summed = term if summed is None else summed + term
    return gelu(layer_norm(summed)).astype(bf16)


def start_assembly(piece_refs, origins, weights_ref, sem):
    tm, stages = lax.axis_index("tm"), lax.axis_size("dp")
    parts = weights_ref.shape[2] // piece_refs[0].shape[2]
    slots = ((piece, first) for piece in piece_refs for first in range(0, piece.shape[0], 2))
    for (piece, first), (even, odd) in zip(slots, origins, strict=True):
        distance = [e if e == o else jnp.where(tm % 2 == 1, o, e) for e, o in zip(even, odd, strict=True)]
        shard = (lax.axis_index("section") ^ distance[0]) * stages + (lax.axis_index("dp") ^ distance[1]) // 2 * 2
        rows = piece.shape[2]
        row = pl.multiple_of(((tm % parts) ^ distance[2]) * rows, ROW_TILE)
        pltpu.make_async_copy(
            piece.at[first : first + 2], weights_ref.at[pl.ds(shard, 2), :, pl.ds(row, rows), :], sem
        ).start()


def own_part_kernel(parts, *refs):
    weights, out, sems = refs[:-2], refs[-2], refs[-1]
    rows = out.shape[1]
    row = pl.multiple_of(lax.axis_index("tm") % parts * rows, ROW_TILE)
    copies = []
    for index, (low, high) in enumerate(taps_between([w.shape[0] for w in weights])):
        source = weights[index].at[:, pl.ds(row, rows), :]
        copies.append(pltpu.make_async_copy(source, out.at[low:high], sems.at[index]))
    for copy in copies:
        copy.start()
    for copy in copies:
        copy.wait()


def layers_kernel(n_pieces, origins, layer_taps, lengths, frames, halo, gain, bias, *rest):
    pieces, out = rest[:n_pieces], rest[n_pieces]
    weights, gain_here, bias_here, *inputs, sem, small_sems = rest[n_pieces + 1 :]
    start_assembly(pieces, origins, weights, sem)
    small = [
        pltpu.make_async_copy(gain, gain_here, small_sems.at[0]),
        pltpu.make_async_copy(bias, bias_here, small_sems.at[1]),
    ]
    for copy in small:
        copy.start()
    length = lengths[0]
    rows, halo_rows = frames.shape[0], halo.shape[0]
    first = lax.axis_index("tm") * rows
    channels = frames.shape[1]

    def masked(values, start):
        index = lax.broadcasted_iota(jnp.int32, (values.shape[0], 1), 0) + start
        return jnp.where(index * 20 < length, values.astype(f32), 0.0)

    x_in = inputs[0]
    put_rows(x_in, 0, masked(frames[...], first))
    put_rows(x_in, rows, masked(halo[...], first + rows))
    put_rows(x_in, rows + halo_rows, jnp.zeros((x_in.shape[1] - rows - halo_rows, channels), f32))
    pltpu.make_async_copy(weights, weights, sem).wait()
    for layer, taps in enumerate(layer_taps[:-1]):
        following = inputs[layer + 1]
        put_rows(following, 0, strided_conv(inputs[layer], weights, taps, following.shape[1]))
    extracted = strided_conv(inputs[-1], weights, layer_taps[-1], out.shape[0]).astype(f32)
    for copy in small:
        copy.wait()
    out[...] = (layer_norm(extracted) * gain_here[...] + bias_here[...]).astype(bf16)


def project_kernel(lengths, project, project_bias, *rest):
    pieces, out, rows_ref = rest[:-2], rest[-2], rest[-1]
    tm = lax.axis_index("tm")
    for index, piece in enumerate(pieces):
        rows = piece.shape[0]
        rows_ref[pl.ds(pl.multiple_of((tm ^ index) * rows, ROW_TILE), rows), :] = piece[...]
    frames, group = out.shape[0], project.shape[0]
    hidden = (dot_nt(rows_ref[...], project[...]) + project_bias[...].astype(f32)).astype(bf16)
    index = lax.broadcasted_iota(jnp.int32, (frames, 1), 0)
    hidden = jnp.where(index * 320 < lengths[0], hidden.astype(f32), 0.0)
    out[...] = jnp.zeros(out.shape, bf16)
    out[:, 0:group] = hidden.astype(bf16)


def position_kernel(n_pieces, own_taps, places, hidden, *rest):
    pieces, out, padded, phases = rest[:n_pieces], rest[n_pieces], rest[n_pieces + 1], rest[n_pieces + 2]
    frames = hidden.shape[0]
    padded[...] = jnp.zeros(padded.shape, f32)
    padded[TAPS // 2 : TAPS // 2 + frames, :] = hidden[...].astype(f32)
    taps, width = pieces[0].shape[0:2]
    span = phases.shape[0]
    for index, piece in enumerate(pieces):
        place, first_tap = places[index]
        shard = (lax.axis_index("section") ^ place[0]) * lax.axis_size("dp") + (lax.axis_index("dp") ^ place[1])
        window = padded[pl.ds(shard * own_taps + first_tap, span), :].astype(bf16)
        term = dot_nt(window, piece[...].reshape(taps * width, piece.shape[2]))
        if index == 0:
            phases[...] = term
        else:
            phases[...] += term
    total = phases[0:frames, 0:width]
    for tap in range(1, taps):
        total = total + phases[tap : tap + frames, tap * width : (tap + 1) * width]
    out[...] = total.astype(out.dtype)


def final_kernel(hidden, mine, theirs, bias, out):
    group = out.shape[0]
    conv = mine[...] + theirs[...].astype(f32)
    position = gelu(conv[:, 0:group] + bias[...])
    out[...] = jnp.transpose(hidden[:, 0:group].astype(f32) + position).astype(bf16)


def taps_between(counts):
    return [(sum(counts[:i]), sum(counts[: i + 1])) for i in range(len(counts))]


def vmem(count):
    return [pl.BlockSpec(memory_space=pltpu.VMEM)] * count


def smem(count):
    return [pl.BlockSpec(memory_space=pltpu.SMEM)] * count


def unplaced(count):
    return [pl.BlockSpec(memory_space=pl.ANY)] * count


LIMIT = pltpu.CompilerParams(vmem_limit_bytes=12 * 1024 * 1024)


def local(
    frames,
    lengths,
    fourth_conv,
    fifth_conv,
    sixth_conv,
    seventh_conv,
    norm_gain,
    norm_bias,
    project_weight,
    project_bias,
    position_weight,
    position_bias,
):
    sections, stages, shares = (lax.axis_size(a) for a in ("section", "dp", "tm"))
    tm = lax.axis_index("tm")
    rows, channels = frames.shape[1:]
    shard_rows = fourth_conv.shape[1]
    parts = max(p for p in (1, 2, 4) if p <= shares and shard_rows % (p * ROW_TILE) == 0)
    part_rows = shard_rows // parts

    group = position_bias.shape[0]
    own_taps = position_weight.shape[1]
    flat_taps, tap_places = [position_weight], [(0, 0, 0)]
    for bit in bits_of(sections):
        flat_taps += [swapped(x, "section", bit) for x in flat_taps]
        tap_places += [flipped(p, "section", bit) for p in tap_places]

    convs = (fourth_conv, fifth_conv, sixth_conv, seventh_conv)
    taps_of = [w.shape[0] for w in convs]
    own = pl.pallas_call(
        functools.partial(own_part_kernel, parts),
        out_shape=jax.ShapeDtypeStruct((sum(taps_of), part_rows, channels), bf16),
        in_specs=unplaced(len(convs)),
        out_specs=pl.BlockSpec(memory_space=pltpu.VMEM),
        scratch_shapes=[pltpu.SemaphoreType.DMA((len(convs),))],
    )(*convs)
    *first, last = paired([own] + [swapped(own, "dp", d) for d in range(1, stages)])
    last = [last]

    def tap_matrices(flat):
        square = flat.reshape(own_taps, group, group)
        return jnp.pad(square, ((0, 0), (0, LANES - group), (0, LANES - group)))

    tap_block = max(own_taps // 2, 1)
    tap_pieces = []
    for flat, place in zip(flat_taps, tap_places, strict=True):
        matrices = tap_matrices(flat)
        tap_pieces += [(matrices[k : k + tap_block], place, k) for k in range(0, own_taps, tap_block)]
    near_count = len(tap_pieces)
    near_taps = [x for x, _, _ in tap_pieces]
    for bit in bits_of(stages)[:-1]:
        tap_pieces += [(swapped(x, "dp", bit), flipped(p, "dp", bit), k) for x, p, k in tap_pieces]
    far_taps = [x for x, _, _ in tap_pieces[near_count:]]
    quarter = -(-len(far_taps) // 4)
    far_quarters = [far_taps[k * quarter : (k + 1) * quarter] for k in range(4)]

    rim = frames[0, :ROW_TILE]
    from_even = lax.ppermute(after(rim, last[0][0], *far_quarters[0]), "tm", [(i, i ^ 1) for i in range(shares)])
    from_odd = lax.ppermute(rim, "tm", [(i, (i + 1 if i % 2 else i - 1) % shares) for i in range(shares)])
    halo = jnp.where(tm % 2 == 0, from_even, jnp.where(tm == shares - 1, jnp.zeros_like(rim), from_odd))

    steps = wide_steps(parts)
    if len(steps) == 2:
        (m1,), (m2,) = first, last
        n1 = sent(m1, steps[0])
        q1 = sent((after(m1[0], *near_taps), m1[1]), steps[1])
        both = joined(n1, m2)
        both = sent((after(both[0], q1[0], from_even), both[1]), steps[1])
        n2 = (both[0][-m2[0].shape[0] :], both[1][-len(m2[1]) :])
        rest = joined(m2, n2)
        rest = sent((after(rest[0], halo, *far_quarters[1]), rest[1]), steps[0])
        pieces = [joined(m1, n1, q1, m2), both, (after(rest[0], *far_quarters[2]), rest[1])]
    else:
        pieces = first + last
        for step in steps:
            pieces = doubled(pieces, step)
    pieces, origins = with_cores(pieces, parts)

    blocks = channels // LANES
    row_counts = [rows + 2 * ROW_TILE, (rows // 2 + 8) // 8 * 8, rows // 4, rows // 8]
    normed = pl.pallas_call(
        functools.partial(layers_kernel, len(pieces), origins, taps_between(taps_of)),
        out_shape=jax.ShapeDtypeStruct((rows // 16, channels), bf16),
        in_specs=smem(1) + vmem(2) + unplaced(2 + len(pieces)),
        out_specs=pl.BlockSpec(memory_space=pltpu.VMEM),
        scratch_shapes=[
            pltpu.VMEM((sections * stages, sum(taps_of), shard_rows, channels), bf16),
            pltpu.VMEM((1, channels), f32),
            pltpu.VMEM((1, channels), f32),
            *(pltpu.VMEM((blocks, count, LANES), f32) for count in row_counts),
            pltpu.SemaphoreType.DMA(()),
            pltpu.SemaphoreType.DMA((2,)),
        ],
        compiler_params=LIMIT,
    )(lengths, frames[0], halo, norm_gain[None], norm_bias[None], *pieces)

    row_pieces = [normed]
    for bit in reversed(bits_of(shares)):
        if bit == 1:
            row_pieces[-1] = after(row_pieces[-1], *far_quarters[3])
        row_pieces += [swapped(x, "tm", bit) for x in row_pieces]
    distance = [0]
    for bit in reversed(bits_of(shares)):
        distance += [d ^ bit for d in distance]
    row_pieces = [x for _, x in sorted(zip(distance, row_pieces), key=lambda pair: pair[0])]
    frame_total = rows * shares // 16

    hidden = pl.pallas_call(
        project_kernel,
        out_shape=jax.ShapeDtypeStruct((frame_total, LANES), bf16),
        in_specs=smem(1) + vmem(2 + len(row_pieces)),
        out_specs=pl.BlockSpec(memory_space=pltpu.VMEM),
        scratch_shapes=[pltpu.VMEM((frame_total, channels), bf16)],
        compiler_params=LIMIT,
    )(lengths, project_weight.T, project_bias, *row_pieces)

    def partial_position(values, kind):
        return pl.pallas_call(
            functools.partial(position_kernel, len(tap_pieces), own_taps, [(p, k) for _, p, k in tap_pieces]),
            out_shape=jax.ShapeDtypeStruct((frame_total, LANES), kind),
            in_specs=vmem(1 + len(tap_pieces)),
            out_specs=pl.BlockSpec(memory_space=pltpu.VMEM),
            scratch_shapes=[
                pltpu.VMEM((frame_total + TAPS + PHASES, LANES), f32),
                pltpu.VMEM((frame_total + PHASES, tap_block * LANES), f32),
            ],
            compiler_params=LIMIT,
        )(values, *(x for x, _, _ in tap_pieces))

    far = stages // 2
    partner_hidden = swapped(hidden, "dp", far)
    mine = partial_position(hidden, f32)
    theirs = swapped(partial_position(after(partner_hidden, mine), bf16), "dp", far)
    encoded = pl.pallas_call(
        final_kernel,
        out_shape=jax.ShapeDtypeStruct((group, frame_total), bf16),
        in_specs=vmem(4),
        out_specs=pl.BlockSpec(memory_space=pltpu.VMEM),
        compiler_params=LIMIT,
    )(hidden, mine, theirs, position_bias[None])
    return encoded[None]


def solution(mesh):
    in_specs = (
        P(SHARDED, "tm", None),
        P(SHARDED),
        P(None, SHARDED, None),
        P(None, SHARDED, None),
        P(None, SHARDED, None),
        P(None, SHARDED, None),
        P(),
        P(),
        P(None, "tm"),
        P(None, "tm"),
        P("tm", SHARDED, None),
        P("tm"),
    )
    out_specs = P(SHARDED, "tm", None)
    return jax.shard_map(local, mesh=mesh, in_specs=in_specs, out_specs=out_specs, check_vma=False)
```

time: 93.5 us -> 69.2 us (0.74)
  starting transfers between devices: 38.9 us -> 23.4 us
  waiting for transfers between devices: 36.3 us -> 32.1 us
  local copies, waits for them, and re-layouts: 5.85 us -> 2.62 us
  Pallas kernels: 10.1 us -> 7.04 us
  other arithmetic: 1.14 us -> 3.01 us
    ppermute x8 -> x4, waiting for transfers between devices: 10.2 us -> 0.96 us  [swapped_by_parity(): return lax.ppermute(x, ('section', 'tm'), pairs)]
    ppermute x18 -> x16, starting transfers between devices: 27.4 us -> 18.8 us  [swapped(): lax.ppermute(x, axis, [(i, i ^ bit) for i in range(lax.axis_size(axis))])]
    ppermute x1 -> x2, waiting for transfers between devices: 0.01 us -> 8.04 us  [the longest x1 7.76 us: local(): lax.ppermute(rim, 'tm', [(i, (i + 1 if i % 2 else i - 1) % shares) for i...]
    ppermute x8 -> x4, starting transfers between devices: 10.2 us -> 4.49 us  [swapped_by_parity(): return lax.ppermute(x, ('section', 'tm'), pairs)]
    pallas_call x5 -> x6, Pallas kernels: 10.1 us -> 7.04 us  [the longest x1 3.03 us: local(): pl.pallas_call(functools.partial(layers_kernel, len(pieces), origins, tap...]
    ppermute x18 -> x16, waiting for transfers between devices: 26 us -> 23.1 us  [swapped(): lax.ppermute(x, axis, [(i, i ^ bit) for i in range(lax.axis_size(axis))])]
    reshape x0 -> x2, local copies, waits for them, and re-layouts: none -> 2.31 us  [tap_matrices(): square = flat.reshape(own_taps, group, group)]
    unnamed x18 -> x14, local copies, waits for them, and re-layouts: 1.95 us -> 0.03 us
  transfers between devices with their start and end apart: 27 -> 22, of which waited for: 13 -> 13; matrix products, arithmetic and copies ran while one was open for 5% -> 8% of each run, Pallas kernels for 8% -> 8%
where the time goes in v3:
time: 69.2 us; the launch traced here: 69 us
  waiting for transfers between devices  32.1 us (46%)
  starting transfers between devices  23.4 us (34%)
  Pallas kernels  7.04 us (10%)
  other arithmetic  3.01 us (4%)
  local copies, waits for them, and re-layouts  2.62 us (4%)
  between operations  0.82 us (1%)
    ppermute x16, waiting for transfers between devices, swapped(): lax.ppermute(x, axis, [(i, i ^ bit) for i in range(lax.axis_size(axis))])  23.1 us
    ppermute x16, starting transfers between devices, swapped(): lax.ppermute(x, axis, [(i, i ^ bit) for i in range(lax.axis_size(axis))])  18.8 us
    ppermute x1, waiting for transfers between devices, local(): lax.ppermute(rim, 'tm', [(i, (i + 1 if i % 2 else i - 1) % shares) for i...  7.76 us
    ppermute x4, starting transfers between devices, swapped_by_parity(): return lax.ppermute(x, ('section', 'tm'), pairs)  4.49 us
    pallas_call x1, Pallas kernels, local(): pl.pallas_call(functools.partial(layers_kernel, len(pieces), origins, tap...  3.03 us
    reshape x2, local copies, waits for them, and re-layouts, tap_matrices(): square = flat.reshape(own_taps, group, group)  2.31 us
    concatenate x3, other arithmetic, joined(): jnp.concatenate([x for x, _ in pieces])  2.2 us
    pallas_call x2, Pallas kernels, partial_position(): pl.pallas_call(functools.partial(position_kernel, len(tap_pieces), own_ta...  1.57 us
  transfers between devices with their start and end apart: 22, of which 13 were waited for; matrix products, arithmetic and copies ran while one was open for 8% of the time, Pallas kernels for 8%

profile of v3, /device:TPU:0, one launch (start us, length us, event | category | flops | bytes accessed | tf_op | source)
XLA Modules:
  0.0 69.0 jit_solution(6301434361554255825)
XLA Ops:
  0.0 2.9 %collective-permute-start.7 = (bf16[1,16,14400]{2,1,0:T(8,128)(2,1)}, bf16[1,16,14400]{2,1,0:T(8,128)(2,1)S(1)}, u32[]{:S(2)}, u32[]{:S(2)}) collective-permute-start(bf16[1,16,14400]{2,1,0:T(8,128)(2,1)} %param.22), channel_id=1, source_target_pairs={{0,16},{16,0},{1,17},{17,1},{2,18},{18,2},{3,19},{19,3},{4,20},{20... | collective-permute-start | bytes 1382408 | tf_op jit(solution)/shard_map/ppermute | solution.py:25
  2.9 1.5 %shard_map.118 = bf16[10,16,512]{2,1,0:T(8,128)(2,1)} custom-call(bf16[3,64,512]{2,1,0:T(8,128)(2,1)} %refs_0_.1, bf16[3,64,512]{2,1,0:T(8,128)(2,1)} %refs_1_.1, bf16[2,64,512]{2,1,0:T(8,128)(2,1)} %refs_2_.1, bf16[2,64,512]{2,1,0:T(8,128)(2,1)} %refs_3_.1), custom_call_target="tpu_custom_call" | custom-call | tf_op jit(solution)/shard_map/pallas_call | solution.py:292
  4.5 1.6 %collective-permute-start.5 = (bf16[10,16,512]{2,1,0:T(8,128)(2,1)}, bf16[10,16,512]{2,1,0:T(8,128)(2,1)S(1)}, u32[]{:S(2)}, u32[]{:S(2)}) collective-permute-start(bf16[10,16,512]{2,1,0:T(8,128)(2,1)} %shard_map.118), channel_id=1, source_target_pairs={{0,1},{1,0},{2,3},{3,2},{4,5},{5,4},{6,7},{7,6},{8,9},{9,8},{10,11... | collective-permute-start | bytes 491528 | tf_op jit(solution)/shard_map/ppermute | solution.py:25
  6.1 2.5 %collective-permute-start = (bf16[10,16,512]{2,1,0:T(8,128)(2,1)}, bf16[10,16,512]{2,1,0:T(8,128)(2,1)S(1)}, u32[]{:S(2)}, u32[]{:S(2)}) collective-permute-start(bf16[10,16,512]{2,1,0:T(8,128)(2,1)} %shard_map.118), channel_id=1, source_target_pairs={{0,3},{1,2},{2,1},{3,0},{4,7},{5,6},{6,5},{7,4},{8,11},{9,10},{10,... | collective-permute-start | bytes 491528 | tf_op jit(solution)/shard_map/ppermute | solution.py:25
  8.7 1.7 %reshape.6 = bf16[16,120,120]{2,1,0:T(8,128)(2,1)S(1)} reshape(bf16[1,16,14400]{2,1,0:T(8,128)(2,1)} %param.22) | data formatting | bytes 921600 | tf_op jit(solution)/shard_map/reshape | solution.py:303
  10.5 1.9 %collective-permute-start.2 = (bf16[8,128,128]{2,1,0:T(8,128)(2,1)S(1)}, bf16[8,128,128]{2,1,0:T(8,128)(2,1)S(1)}, u32[]{:S(2)}, u32[]{:S(2)}) collective-permute-start(bf16[8,128,128]{2,1,0:T(8,128)(2,1)S(1)} %get-tuple-element.22.rest_0_), channel_id=1, source_target_pairs={{0,1},{1,0},{2,3},{3,2},{4,5},{5,4},{6,7},{7,6},{8,9},{9,8},{10,11... | collective-permute-start | bytes 786440 | tf_op jit(solution)/shard_map/ppermute | solution.py:25
  14.5 1.8 %collective-permute-start.8 = (bf16[2,10,16,512]{3,2,1,0:T(8,128)(2,1)}, bf16[2,10,16,512]{3,2,1,0:T(8,128)(2,1)}, u32[]{:S(2)}, u32[]{:S(2)}) collective-permute-start(bf16[2,10,16,512]{3,2,1,0:T(8,128)(2,1)} %maximum_select_fusion.1), channel_id=1, source_target_pairs={{0,8},{4,20},{8,0},{12,28},{16,24},{20,4},{24,16},{28,12},{1,9},{5... | collective-permute-start | bytes 983048 | tf_op jit(solution)/shard_map/ppermute | solution.py:36
  16.4 1.1 %collective-permute-done = bf16[10,16,512]{2,1,0:T(8,128)(2,1)S(1)} collective-permute-done((bf16[10,16,512]{2,1,0:T(8,128)(2,1)}, bf16[10,16,512]{2,1,0:T(8,128)(2,1)S(1)}, u32[]{:S(2)}, u32[]{:S(2)}) %collective-permute-start) | collective-permute-done | bytes 163872 | tf_op jit(solution)/shard_map/ppermute | solution.py:25
  17.5 5.7 %collective-permute-done.1 = bf16[10,16,512]{2,1,0:T(8,128)(2,1)S(1)} collective-permute-done((bf16[10,16,512]{2,1,0:T(8,128)(2,1)}, bf16[10,16,512]{2,1,0:T(8,128)(2,1)S(1)}, u32[]{:S(2)}, u32[]{:S(2)}) %collective-permute-start.1) | collective-permute-done | bytes 163872 | tf_op jit(solution)/shard_map/ppermute | solution.py:25
  24.0 0.9 %pad_maximum_fusion.1 = bf16[4,10,16,512]{3,2,1,0:T(8,128)(2,1)} fusion(bf16[2,10,16,512]{3,2,1,0:T(8,128)(2,1)S(1)} %maximum_select_fusion, bf16[2,10,16,512]{3,2,1,0:T(8,128)(2,1)S(1)} %collective-permute-done.6), kind=kLoop, calls=%fused_computation.1 | loop fusion | flops 327680 | bytes 1310720 | tf_op jit(solution)/shard_map/concatenate | solution.py:90
  25.2 1.5 %collective-permute-start.9 = (bf16[4,10,16,512]{3,2,1,0:T(8,128)(2,1)}, bf16[4,10,16,512]{3,2,1,0:T(8,128)(2,1)S(1)}, u32[]{:S(2)}, u32[]{:S(2)}) collective-permute-start(bf16[4,10,16,512]{3,2,1,0:T(8,128)(2,1)} %pad_maximum_fusion.1), channel_id=1, source_target_pairs={{0,8},{4,20},{8,0},{12,28},{16,24},{20,4},{24,16},{28,12},{1,9},{5... | collective-permute-start | bytes 1966088 | tf_op jit(solution)/shard_map/ppermute | solution.py:36
  27.4 7.8 %collective-permute-done.4 = bf16[16,512]{1,0:T(8,128)(2,1)S(1)} collective-permute-done((bf16[16,512]{1,0:T(8,128)(2,1)S(1)}, bf16[16,512]{1,0:T(8,128)(2,1)S(1)}, u32[]{:S(2)}, u32[]{:S(2)}) %collective-permute-start.4) | collective-permute-done | bytes 16416 | tf_op jit(solution)/shard_map/ppermute | solution.py:321
  35.2 1.0 %collective-permute-done.9.rest_1_ = bf16[4,10,16,512]{3,2,1,0:T(8,128)(2,1)S(1)} collective-permute-done((bf16[4,10,16,512]{3,2,1,0:T(8,128)(2,1)}, bf16[4,10,16,512]{3,2,1,0:T(8,128)(2,1)S(1)}, u32[]{:S(2)}, u32[]{:S(2)}) %collective-permute-start.9) | collective-permute-done | bytes 655392 | tf_op jit(solution)/shard_map/ppermute | solution.py:36
  36.9 1.2 %pad_maximum_fusion.rest_0_ = bf16[8,10,16,512]{3,2,1,0:T(8,128)(2,1)S(1)} fusion(bf16[2,10,16,512]{3,2,1,0:T(8,128)(2,1)S(1)} %maximum_select_fusion, bf16[2,10,16,512]{3,2,1,0:T(8,128)(2,1)} %collective-permute-done.8, bf16[2,10,16,512]{3,2,1,0:T(8,128)(2,1)S(1)} %collective-permute-done.6, bf16[2,10,16,512]{3,2,1,0:T(8,128)(2,1)} %maximum_select_fusion.1), kind=kLoop, calls=%fused_computation | loop fusion | flops 1966080 | bytes 2621440 | tf_op jit(solution)/shard_map/concatenate | solution.py:90
  39.5 7.7 %collective-permute-done.12.rest_6_ = bf16[8,128,128]{2,1,0:T(8,128)(2,1)S(1)} collective-permute-done((bf16[8,128,128]{2,1,0:T(8,128)(2,1)S(1)}, bf16[8,128,128]{2,1,0:T(8,128)(2,1)S(1)}, u32[]{:S(2)}, u32[]{:S(2)}) %collective-permute-start.12) | collective-permute-done | bytes 262176 | tf_op jit(solution)/shard_map/ppermute | solution.py:25
  48.5 0.8 %collective-permute-done.15.rest_5_ = bf16[4,10,16,512]{3,2,1,0:T(8,128)(2,1)S(1)} collective-permute-done((bf16[4,10,16,512]{3,2,1,0:T(8,128)(2,1)S(1)}, bf16[4,10,16,512]{3,2,1,0:T(8,128)(2,1)S(1)}, u32[]{:S(2)}, u32[]{:S(2)}) %collective-permute-start.15) | collective-permute-done | bytes 655392 | tf_op jit(solution)/shard_map/ppermute | solution.py:25
  49.3 3.0 %shard_map.119.rest_0_ = bf16[32,512]{1,0:T(8,128)(2,1)S(1)} custom-call(s32[1]{0:T(128)S(6)} %copy.13.lengths, bf16[512,512]{1,0:T(8,128)(2,1)S(1)} %bitcast.12, bf16[16,512]{1,0:T(8,128)(2,1)S(1)} %select_select_fusion.halo, f32[1,512]{1,0:T(1,128)S(1)} %bitcast.14, f32[1,512]{1,0:T(1,128)S(1)} %bitcast.15, ...), custom_call_target="tpu_custom_call" | custom-call | tf_op jit(solution)/shard_map/pallas_call | solution.py:343
  52.3 1.2 %collective-permute-start.17 = (bf16[32,512]{1,0:T(8,128)(2,1)S(1)}, bf16[32,512]{1,0:T(8,128)(2,1)S(1)}, u32[]{:S(2)}, u32[]{:S(2)}) collective-permute-start(bf16[32,512]{1,0:T(8,128)(2,1)S(1)} %shard_map.119.rest_0_), channel_id=1, source_target_pairs={{0,8},{4,12},{8,0},{12,4},{1,9},{5,13},{9,1},{13,5},{2,10},{6,14},... | collective-permute-start | bytes 98312 | tf_op jit(solution)/shard_map/ppermute | solution.py:25
  53.5 2.4 %collective-permute-done.18.rest_7_ = bf16[8,128,128]{2,1,0:T(8,128)(2,1)S(1)} collective-permute-done((bf16[8,128,128]{2,1,0:T(8,128)(2,1)S(1)}, bf16[8,128,128]{2,1,0:T(8,128)(2,1)S(1)}, u32[]{:S(2)}, u32[]{:S(2)}) %collective-permute-start.18) | collective-permute-done | bytes 262176 | tf_op jit(solution)/shard_map/ppermute | solution.py:25
  56.3 1.2 %collective-permute-done.19.rest_3_ = bf16[32,512]{1,0:T(8,128)(2,1)S(1)} collective-permute-done((bf16[32,512]{1,0:T(8,128)(2,1)S(1)}, bf16[32,512]{1,0:T(8,128)(2,1)S(1)}, u32[]{:S(2)}, u32[]{:S(2)}) %collective-permute-start.19) | collective-permute-done | bytes 32800 | tf_op jit(solution)/shard_map/ppermute | solution.py:25
  57.7 2.9 %collective-permute-start.20 = (bf16[128,128]{1,0:T(8,128)(2,1)S(1)}, bf16[128,128]{1,0:T(8,128)(2,1)S(1)}, u32[]{:S(2)}, u32[]{:S(2)}) collective-permute-start(bf16[128,128]{1,0:T(8,128)(2,1)S(1)} %shard_map.120.hidden), channel_id=1, source_target_pairs={{0,2},{1,3},{2,0},{3,1},{4,6},{5,7},{6,4},{7,5},{8,10},{9,11},{10,... | collective-permute-start | bytes 98312 | tf_op jit(solution)/shard_map/ppermute | solution.py:25
  61.4 1.1 %collective-permute-done.20.hidden = bf16[128,128]{1,0:T(8,128)(2,1)S(1)} collective-permute-done((bf16[128,128]{1,0:T(8,128)(2,1)S(1)}, bf16[128,128]{1,0:T(8,128)(2,1)S(1)}, u32[]{:S(2)}, u32[]{:S(2)}) %collective-permute-start.20) | collective-permute-done | bytes 32800 | tf_op jit(solution)/shard_map/ppermute | solution.py:25
  63.4 2.9 %collective-permute-start.21 = (bf16[128,128]{1,0:T(8,128)(2,1)S(1)}, bf16[128,128]{1,0:T(8,128)(2,1)S(1)}, u32[]{:S(2)}, u32[]{:S(2)}) collective-permute-start(bf16[128,128]{1,0:T(8,128)(2,1)S(1)} %shard_map.122), channel_id=1, source_target_pairs={{0,2},{1,3},{2,0},{3,1},{4,6},{5,7},{6,4},{7,5},{8,10},{9,11},{10,... | collective-permute-start | bytes 98312 | tf_op jit(solution)/shard_map/ppermute | solution.py:25
  66.3 1.9 %collective-permute-done.21.theirs = bf16[128,128]{1,0:T(8,128)(2,1)S(1)} collective-permute-done((bf16[128,128]{1,0:T(8,128)(2,1)S(1)}, bf16[128,128]{1,0:T(8,128)(2,1)S(1)}, u32[]{:S(2)}, u32[]{:S(2)}) %collective-permute-start.21) | collective-permute-done | bytes 32800 | tf_op jit(solution)/shard_map/ppermute | solution.py:25
  (52 shorter events, 9.8 us)
Async XLA Ops:
  0.0 13.8 %collective-permute-start.7 = (bf16[1,16,14400]{2,1,0:T(8,128)(2,1)}, bf16[1,16,14400]{2,1,0:T(8,128)(2,1)S(1)}, u32[]{:S(2)}, u32[]{:S(2)}) collective-permute-start(bf16[1,16,14400]{2,1,0:T(8,128)(2,1)} %param.22), channel_id=1, source_target_pairs={{0,16},{16,0},{1,17},{17,1},{2,18},{18,2},{3,19},{19,3},{4,20},{20... | collective-permute-start | bytes 1382408 | tf_op jit(solution)/shard_map/ppermute | solution.py:25
  4.5 7.9 %collective-permute-start.5 = (bf16[10,16,512]{2,1,0:T(8,128)(2,1)}, bf16[10,16,512]{2,1,0:T(8,128)(2,1)S(1)}, u32[]{:S(2)}, u32[]{:S(2)}) collective-permute-start(bf16[10,16,512]{2,1,0:T(8,128)(2,1)} %shard_map.118), channel_id=1, source_target_pairs={{0,1},{1,0},{2,3},{3,2},{4,5},{5,4},{6,7},{7,6},{8,9},{9,8},{10,11... | collective-permute-start | bytes 491528 | tf_op jit(solution)/shard_map/ppermute | solution.py:25
  6.1 11.4 %collective-permute-start = (bf16[10,16,512]{2,1,0:T(8,128)(2,1)}, bf16[10,16,512]{2,1,0:T(8,128)(2,1)S(1)}, u32[]{:S(2)}, u32[]{:S(2)}) collective-permute-start(bf16[10,16,512]{2,1,0:T(8,128)(2,1)} %shard_map.118), channel_id=1, source_target_pairs={{0,3},{1,2},{2,1},{3,0},{4,7},{5,6},{6,5},{7,4},{8,11},{9,10},{10,... | collective-permute-start | bytes 491528 | tf_op jit(solution)/shard_map/ppermute | solution.py:25
  8.6 14.6 %collective-permute-start.1 = (bf16[10,16,512]{2,1,0:T(8,128)(2,1)}, bf16[10,16,512]{2,1,0:T(8,128)(2,1)S(1)}, u32[]{:S(2)}, u32[]{:S(2)}) collective-permute-start(bf16[10,16,512]{2,1,0:T(8,128)(2,1)} %shard_map.118), channel_id=1, source_target_pairs={{0,2},{1,3},{2,0},{3,1},{4,6},{5,7},{6,4},{7,5},{8,10},{9,11},{10,... | collective-permute-start | bytes 491528 | tf_op jit(solution)/shard_map/ppermute | solution.py:25
  10.5 13.5 %collective-permute-start.2 = (bf16[8,128,128]{2,1,0:T(8,128)(2,1)S(1)}, bf16[8,128,128]{2,1,0:T(8,128)(2,1)S(1)}, u32[]{:S(2)}, u32[]{:S(2)}) collective-permute-start(bf16[8,128,128]{2,1,0:T(8,128)(2,1)S(1)} %get-tuple-element.22.rest_0_), channel_id=1, source_target_pairs={{0,1},{1,0},{2,3},{3,2},{4,5},{5,4},{6,7},{7,6},{8,9},{9,8},{10,11... | collective-permute-start | bytes 786440 | tf_op jit(solution)/shard_map/ppermute | solution.py:25
  13.2 10.8 %collective-permute-start.6 = (bf16[2,10,16,512]{3,2,1,0:T(8,128)(2,1)}, bf16[2,10,16,512]{3,2,1,0:T(8,128)(2,1)S(1)}, u32[]{:S(2)}, u32[]{:S(2)}) collective-permute-start(bf16[2,10,16,512]{3,2,1,0:T(8,128)(2,1)} %maximum_select_fusion.1), channel_id=1, source_target_pairs={{0,16},{4,12},{8,24},{12,4},{16,0},{20,28},{24,8},{28,20},{1,17},{... | collective-permute-start | bytes 983048 | tf_op jit(solution)/shard_map/ppermute | solution.py:36
  14.5 10.7 %collective-permute-start.8 = (bf16[2,10,16,512]{3,2,1,0:T(8,128)(2,1)}, bf16[2,10,16,512]{3,2,1,0:T(8,128)(2,1)}, u32[]{:S(2)}, u32[]{:S(2)}) collective-permute-start(bf16[2,10,16,512]{3,2,1,0:T(8,128)(2,1)} %maximum_select_fusion.1), channel_id=1, source_target_pairs={{0,8},{4,20},{8,0},{12,28},{16,24},{20,4},{24,16},{28,12},{1,9},{5... | collective-permute-start | bytes 983048 | tf_op jit(solution)/shard_map/ppermute | solution.py:36
  24.0 1.2 %collective-permute-start.3 = (bf16[16,512]{1,0:T(8,128)(2,1)S(1)}, bf16[16,512]{1,0:T(8,128)(2,1)S(1)}, u32[]{:S(2)}, u32[]{:S(2)}) collective-permute-start(bf16[16,512]{1,0:T(8,128)(2,1)S(1)} %slice_bitcast_fusion), channel_id=1, source_target_pairs={{0,4},{4,0},{8,12},{12,8},{1,5},{5,1},{9,13},{13,9},{2,6},{6,2},{1... | collective-permute-start | bytes 49160 | tf_op jit(solution)/shard_map/ppermute | solution.py:320
  25.2 11.0 %collective-permute-start.9 = (bf16[4,10,16,512]{3,2,1,0:T(8,128)(2,1)}, bf16[4,10,16,512]{3,2,1,0:T(8,128)(2,1)S(1)}, u32[]{:S(2)}, u32[]{:S(2)}) collective-permute-start(bf16[4,10,16,512]{3,2,1,0:T(8,128)(2,1)} %pad_maximum_fusion.1), channel_id=1, source_target_pairs={{0,8},{4,20},{8,0},{12,28},{16,24},{20,4},{24,16},{28,12},{1,9},{5... | collective-permute-start | bytes 1966088 | tf_op jit(solution)/shard_map/ppermute | solution.py:36
  26.7 8.5 %collective-permute-start.4 = (bf16[16,512]{1,0:T(8,128)(2,1)S(1)}, bf16[16,512]{1,0:T(8,128)(2,1)S(1)}, u32[]{:S(2)}, u32[]{:S(2)}) collective-permute-start(bf16[16,512]{1,0:T(8,128)(2,1)S(1)} %slice_bitcast_fusion), channel_id=1, source_target_pairs={{0,12},{4,8},{8,4},{12,0},{1,13},{5,9},{9,5},{13,1},{2,14},{6,10},... | collective-permute-start | bytes 49160 | tf_op jit(solution)/shard_map/ppermute | solution.py:321
  26.8 9.5 %collective-permute-start.10 = (bf16[8,128,128]{2,1,0:T(8,128)(2,1)S(1)}, bf16[8,128,128]{2,1,0:T(8,128)(2,1)S(1)}, u32[]{:S(2)}, u32[]{:S(2)}) collective-permute-start(bf16[8,128,128]{2,1,0:T(8,128)(2,1)S(1)} %get-tuple-element.21.rest_1_), channel_id=1, source_target_pairs={{0,1},{1,0},{2,3},{3,2},{4,5},{5,4},{6,7},{7,6},{8,9},{9,8},{10,11... | collective-permute-start | bytes 786440 | tf_op jit(solution)/shard_map/ppermute | solution.py:25
  36.3 13.0 %copy-start.2 = (f32[512]{0:T(512)S(1)}, f32[512]{0:T(512)}, u32[]{:S(2)}) copy-start(f32[512]{0:T(512)} %param.18) | copy-start | bytes 6148
  36.3 13.0 %copy-start.3 = (f32[512]{0:T(512)S(1)}, f32[512]{0:T(512)}, u32[]{:S(2)}) copy-start(f32[512]{0:T(512)} %param.19) | copy-start | bytes 6148
  36.3 10.9 %collective-permute-start.11 = (bf16[4,10,16,512]{3,2,1,0:T(8,128)(2,1)S(1)}, bf16[4,10,16,512]{3,2,1,0:T(8,128)(2,1)S(1)}, u32[]{:S(2)}, u32[]{:S(2)}) collective-permute-start(bf16[4,10,16,512]{3,2,1,0:T(8,128)(2,1)S(1)} %pad_maximum_fusion.2), channel_id=1, source_target_pairs={{0,16},{4,12},{8,24},{12,4},{16,0},{20,28},{24,8},{28,20},{1,17},{... | collective-permute-start | bytes 1966088 | tf_op jit(solution)/shard_map/ppermute | solution.py:36
  38.1 10.3 %collective-permute-start.13 = (bf16[8,10,16,512]{3,2,1,0:T(8,128)(2,1)S(1)}, bf16[8,10,16,512]{3,2,1,0:T(8,128)(2,1)S(1)}, u32[]{:S(2)}, u32[]{:S(2)}) collective-permute-start(bf16[8,10,16,512]{3,2,1,0:T(8,128)(2,1)S(1)} %pad_maximum_fusion.rest_0_), channel_id=1, source_target_pairs={{0,4},{4,0},{8,12},{12,8},{1,5},{5,1},{9,13},{13,9},{2,6},{6,2},{1... | collective-permute-start | bytes 3932168 | tf_op jit(solution)/shard_map/ppermute | solution.py:25
  38.9 8.3 %collective-permute-start.12 = (bf16[8,128,128]{2,1,0:T(8,128)(2,1)S(1)}, bf16[8,128,128]{2,1,0:T(8,128)(2,1)S(1)}, u32[]{:S(2)}, u32[]{:S(2)}) collective-permute-start(bf16[8,128,128]{2,1,0:T(8,128)(2,1)S(1)} %get-tuple-element.20.rest_2_), channel_id=1, source_target_pairs={{0,1},{1,0},{2,3},{3,2},{4,5},{5,4},{6,7},{7,6},{8,9},{9,8},{10,11... | collective-permute-start | bytes 786440 | tf_op jit(solution)/shard_map/ppermute | solution.py:25
  39.5 9.0 %collective-permute-start.14 = (bf16[4,10,16,512]{3,2,1,0:T(8,128)(2,1)S(1)}, bf16[4,10,16,512]{3,2,1,0:T(8,128)(2,1)S(1)}, u32[]{:S(2)}, u32[]{:S(2)}) collective-permute-start(bf16[4,10,16,512]{3,2,1,0:T(8,128)(2,1)S(1)} %collective-permute-done.9.rest_1_), channel_id=1, source_target_pairs={{0,4},{4,0},{8,12},{12,8},{1,5},{5,1},{9,13},{13,9},{2,6},{6,2},{1... | collective-permute-start | bytes 1966088 | tf_op jit(solution)/shard_map/ppermute | solution.py:25
  47.2 2.1 %collective-permute-start.15 = (bf16[4,10,16,512]{3,2,1,0:T(8,128)(2,1)S(1)}, bf16[4,10,16,512]{3,2,1,0:T(8,128)(2,1)S(1)}, u32[]{:S(2)}, u32[]{:S(2)}) collective-permute-start(bf16[4,10,16,512]{3,2,1,0:T(8,128)(2,1)S(1)} %collective-permute-done.11.rest_2_), channel_id=1, source_target_pairs={{0,4},{4,0},{8,12},{12,8},{1,5},{5,1},{9,13},{13,9},{2,6},{6,2},{1... | collective-permute-start | bytes 1966088 | tf_op jit(solution)/shard_map/ppermute | solution.py:25
  47.2 8.7 %collective-permute-start.18 = (bf16[8,128,128]{2,1,0:T(8,128)(2,1)S(1)}, bf16[8,128,128]{2,1,0:T(8,128)(2,1)S(1)}, u32[]{:S(2)}, u32[]{:S(2)}) collective-permute-start(bf16[8,128,128]{2,1,0:T(8,128)(2,1)S(1)} %get-tuple-element.19.rest_3_), channel_id=1, source_target_pairs={{0,1},{1,0},{2,3},{3,2},{4,5},{5,4},{6,7},{7,6},{8,9},{9,8},{10,11... | collective-permute-start | bytes 786440 | tf_op jit(solution)/shard_map/ppermute | solution.py:25
  52.3 4.0 %collective-permute-start.17 = (bf16[32,512]{1,0:T(8,128)(2,1)S(1)}, bf16[32,512]{1,0:T(8,128)(2,1)S(1)}, u32[]{:S(2)}, u32[]{:S(2)}) collective-permute-start(bf16[32,512]{1,0:T(8,128)(2,1)S(1)} %shard_map.119.rest_0_), channel_id=1, source_target_pairs={{0,8},{4,12},{8,0},{12,4},{1,9},{5,13},{9,1},{13,5},{2,10},{6,14},... | collective-permute-start | bytes 98312 | tf_op jit(solution)/shard_map/ppermute | solution.py:25
  53.5 2.8 %collective-permute-start.16 = (bf16[32,512]{1,0:T(8,128)(2,1)S(1)}, bf16[32,512]{1,0:T(8,128)(2,1)S(1)}, u32[]{:S(2)}, u32[]{:S(2)}) collective-permute-start(bf16[32,512]{1,0:T(8,128)(2,1)S(1)} %shard_map.119.rest_0_), channel_id=1, source_target_pairs={{0,4},{4,0},{8,12},{12,8},{1,5},{5,1},{9,13},{13,9},{2,6},{6,2},{1... | collective-permute-start | bytes 98312 | tf_op jit(solution)/shard_map/ppermute | solution.py:25
  56.3 1.2 %collective-permute-start.19 = (bf16[32,512]{1,0:T(8,128)(2,1)S(1)}, bf16[32,512]{1,0:T(8,128)(2,1)S(1)}, u32[]{:S(2)}, u32[]{:S(2)}) collective-permute-start(bf16[32,512]{1,0:T(8,128)(2,1)S(1)} %collective-permute-done.17.rest_2_), channel_id=1, source_target_pairs={{0,4},{4,0},{8,12},{12,8},{1,5},{5,1},{9,13},{13,9},{2,6},{6,2},{1... | collective-permute-start | bytes 98312 | tf_op jit(solution)/shard_map/ppermute | solution.py:25
  57.7 4.9 %collective-permute-start.20 = (bf16[128,128]{1,0:T(8,128)(2,1)S(1)}, bf16[128,128]{1,0:T(8,128)(2,1)S(1)}, u32[]{:S(2)}, u32[]{:S(2)}) collective-permute-start(bf16[128,128]{1,0:T(8,128)(2,1)S(1)} %shard_map.120.hidden), channel_id=1, source_target_pairs={{0,2},{1,3},{2,0},{3,1},{4,6},{5,7},{6,4},{7,5},{8,10},{9,11},{10,... | collective-permute-start | bytes 98312 | tf_op jit(solution)/shard_map/ppermute | solution.py:25
  63.4 4.9 %collective-permute-start.21 = (bf16[128,128]{1,0:T(8,128)(2,1)S(1)}, bf16[128,128]{1,0:T(8,128)(2,1)S(1)}, u32[]{:S(2)}, u32[]{:S(2)}) collective-permute-start(bf16[128,128]{1,0:T(8,128)(2,1)S(1)} %shard_map.122), channel_id=1, source_target_pairs={{0,2},{1,3},{2,0},{3,1},{4,6},{5,7},{6,4},{7,5},{8,10},{9,11},{10,... | collective-permute-start | bytes 98312 | tf_op jit(solution)/shard_map/ppermute | solution.py:25
  (5 other events, 35.2 us)
